TPU v7x, 512 devices: a whole 4x4x16 slice. The times are simulated.
512 devices in a mesh: box: 32 (over z_lo, y), dir: 16 (over x, z_hi, core).
Axes of the slice: x: 4, y: 4, z: 16 (z_hi: 2, z_lo: 8; z = z_hi * 8 + z_lo), core: 2. Of those that a mesh axis runs over, the one named last changes fastest.
Arguments:
- source: bfloat16 [64, 2, 2, 256, 128], P(None, None, None, 'box'), may hold values from -6 to 6
- near_blocks: bfloat16 [27, 2, 64, 64], P(None, None, 'dir'), may hold values from -0.109375 to 0.109375
- near_mask: int32 [27, 256, 128], P(None, 'box'), may hold values 0 or 1
- radiate: bfloat16 [2, 8, 16, 64], P(None, None, 'dir'), may hold values from -0.5 to 0.5
- receive: bfloat16 [2, 8, 16, 64], P(None, None, None, 'dir'), may hold values from -0.375 to 0.375
- theta_one: float32 [16, 8], replicated, may hold values from -0.75 to 0.75
- theta_two: float32 [32, 16], replicated, may hold values from -0.5 to 0.5
- theta_three: float32 [64, 32], replicated, may hold values from -0.375 to 0.375
- phi_taps: float32 [3, 2, 3], replicated, may hold values from -3.5 to 3.5
- shift_one: float32 [8, 16, 32], P(None, None, 'dir'), may hold values from -3.140625 to 3.140625
- shift_two: float32 [8, 32, 64], P(None, None, 'dir'), may hold values from -3.140625 to 3.140625
- shift_three: float32 [8, 64, 128], P(None, None, 'dir'), may hold values from -3.140625 to 3.140625
- trans_one: float32 [32, 2, 16, 32], P(None, None, None, 'dir'), may hold values from -0.75 to 0.75
- trans_two: float32 [32, 2, 32, 64], P(None, None, None, 'dir'), may hold values from -0.75 to 0.75
- trans_three: float32 [32, 2, 64, 128], P(None, None, None, 'dir'), may hold values from -0.75 to 0.75
- far_lists: int32 [3, 32, 3], replicated, may hold values from -2 to 2, as said below
Outputs:
- product: float32 [64, 2, 2, 256, 128], P('dir', None, None, 'box')
Inputs may be any that keep to these rules, and one draw needn't show every extreme that they name: `far_lists`: for each of the 3 levels the 32 rows are distinct offsets (dx, dy, dz) with every component in -2..2 and at least one component equal to -2 or 2; each level's list holds (-2, 0, 0) and (2, 0, 0).
All inputs are finite; a program needn't handle non-finite values. No bound on the sum of `near_mask` on one device may be relied on, other than what follows from the above.
Results may differ from a plain program's by a relative error of at most 0.0003.
Values may be sent and summed in bfloat16 or wider, within the bound.
A program may use at most 128 MiB of HBM per device.

v0:
```python
import jax
import jax.numpy as jnp
import numpy as np
from jax import lax
from jax.sharding import PartitionSpec as P

NT0 = 8
GY = 8
GZ = 16


HIGHEST = lax.Precision.HIGHEST


def padded_2(cells, sides, width, closed):
    for axis, dim in sides:
        count = lax.axis_size(axis)
        ends = count if closed else count - 1
        head = lax.slice_in_dim(cells, 0, width, axis=dim)
        tail = lax.slice_in_dim(cells, cells.shape[dim] - width, cells.shape[dim], axis=dim)
        cells = jnp.concatenate(
            [
                lax.ppermute(tail, axis, [(i, (i + 1) % count) for i in range(ends)]),
                cells,
                lax.ppermute(head, axis, [((i + 1) % count, i) for i in range(ends)]),
            ],
            axis=dim,
        )
    return cells


def phi_rim(pattern):
    return padded_2(pattern, (("dir", 3),), 1, True)


def phi_up_from(pattern, extended, taps):
    count = pattern.shape[3]
    trailing = (1,) * (pattern.ndim - 4)
    doubled = jnp.repeat(extended, 2, axis=3)
    weights = jnp.tile(taps, (count, 1))
    result = jnp.zeros(pattern.shape[:3] + (2 * count,) + pattern.shape[4:], jnp.float32)
    for tap_index in range(3):
        window = doubled[:, :, :, 2 * tap_index : 2 * tap_index + 2 * count]
        result = result + weights[:, tap_index].reshape((1, 1, 1, -1) + trailing) * window
    return result


def phi_up(pattern, taps):
    return phi_up_from(pattern, phi_rim(pattern), taps)


def phi_down(pattern, taps):
    count = pattern.shape[3] // 2
    trailing = (1,) * (pattern.ndim - 4)
    pieces = []
    for tap_index in range(3):
        weighted = jnp.tile(taps[:, tap_index], count).reshape((1, 1, 1, -1) + trailing) * pattern
        pieces.append(
            weighted.reshape(pattern.shape[:3] + (count, 2) + pattern.shape[4:]).sum(axis=4)
        )
    stacked = jnp.concatenate(pieces, axis=0)
    extended = phi_rim(stacked)
    result = jnp.zeros(pattern.shape[:3] + (count,) + pattern.shape[4:], jnp.float32)
    for tap_index in range(3):
        result = (
            result
            + extended[
                2 * tap_index : 2 * tap_index + 2, :, :, 2 - tap_index : 2 - tap_index + count
            ]
        )
    return result


def theta_boxes(matrix, pattern):
    return jnp.einsum("st,crtpb->crspb", matrix, pattern, precision=HIGHEST)


def theta_boxes_back(matrix, pattern):
    return jnp.einsum("st,crspb->crtpb", matrix, pattern, precision=HIGHEST)


def theta_upper(matrix, pattern):
    return jnp.einsum("st,crbpt->crbps", matrix, pattern, precision=HIGHEST)


def theta_upper_back(matrix, pattern):
    return jnp.einsum("st,crbps->crbpt", matrix, pattern, precision=HIGHEST)


def turn_phase(pattern, cosine, sine, sign):
    real_part = pattern[0] * cosine - sign * pattern[1] * sine
    imag_part = pattern[1] * cosine + sign * pattern[0] * sine
    return jnp.stack([real_part, imag_part])


def child_kinds(layers, rows_y, rows_z):
    index = np.arange(layers * rows_y * rows_z)
    along_x = index // (rows_y * rows_z)
    along_y = index // rows_z % rows_y
    along_z = index % rows_z
    kinds = 4 * (along_x % 2) + 2 * (along_y % 2) + along_z % 2
    return (kinds[None, :] == np.arange(8)[:, None]).astype(np.float32)


def phase_tables(angles, layers, rows_y, rows_z):
    onehot = jnp.asarray(child_kinds(layers, rows_y, rows_z))
    phase = jnp.einsum("otp,ob->tpb", angles, onehot, precision=HIGHEST)
    return (jnp.cos(phase), jnp.sin(phase))


def block_table(plane, row_len, group):
    index = np.arange(2 * group * plane)
    layer_local = index // plane
    along_y = index % plane // row_len
    along_z = index % row_len
    target = layer_local // 2 * (plane // 4) + along_y // 2 * (row_len // 2) + along_z // 2
    return (target[:, None] == np.arange(group * plane // 4)[None, :]).astype(np.float32)


def parent_table(layers, rows_y, rows_z):
    index = np.arange(layers * rows_y * rows_z)
    along_x = index // (rows_y * rows_z)
    along_y = index // rows_z % rows_y
    along_z = index % rows_z
    half_y = rows_y // 2
    half_z = rows_z // 2
    target = along_x // 2 * (half_y * half_z) + along_y // 2 * half_z + along_z // 2
    return (target[:, None] == np.arange(layers // 2 * half_y * half_z)[None, :]).astype(np.float32)


def combine_pairs(products):
    return jnp.stack([products[0, 0] - products[1, 1], products[0, 1] + products[1, 0]])


def translate_flat(extended, table, offsets, plane, row_len):
    count = extended.shape[4] - 4 * plane
    margin = 2 * row_len + 2
    padded = jnp.pad(extended, ((0, 0),) * 4 + ((margin, margin),))
    index = jnp.arange(count, dtype=jnp.int32)
    along_y = index // row_len % (plane // row_len)
    along_z = index % row_len

    def window(offset):
        start = margin + (offset[0] + 2) * plane + offset[1] * row_len + offset[2]
        piece = lax.dynamic_slice_in_dim(padded, start, count, 4)
        moved_y = along_y + offset[1]
        moved_z = along_z + offset[2]
        valid = (moved_y >= 0) & (moved_y < plane // row_len) & (moved_z >= 0) & (moved_z < row_len)
        return piece * valid.astype(jnp.float32)

    stacked = jax.vmap(window)(offsets)
    products = jnp.einsum("kctp,kdrtpb->cdrtpb", table, stacked, precision=HIGHEST)
    return combine_pairs(products)


def translate_upper(extended, table, offsets):
    padded = jnp.pad(extended, ((0, 0),) * 3 + ((2, 2), (2, 2), (0, 0)))
    shape_out = extended.shape[:2] + (extended.shape[2] - 4,) + extended.shape[3:]
    zero = jnp.int32(0)

    def window(offset):
        start = (zero, zero, offset[0] + 2, offset[1] + 2, offset[2] + 2, zero)
        return lax.dynamic_slice(padded, start, shape_out)

    stacked = jax.vmap(window)(offsets)
    products = jnp.einsum("kcq,kdrxyzq->cdrxyzq", table, stacked, precision=HIGHEST)
    return combine_pairs(products)


def complex_rows(columns, pattern):
    form = "tnu,rtnb->urb"
    real_part = jnp.einsum(form, columns[0], pattern[0], precision=HIGHEST) - jnp.einsum(
        form, columns[1], pattern[1], precision=HIGHEST
    )
    imag_part = jnp.einsum(form, columns[0], pattern[1], precision=HIGHEST) + jnp.einsum(
        form, columns[1], pattern[0], precision=HIGHEST
    )
    return jnp.stack([real_part, imag_part], axis=1)


def leaf_pattern(table, source_flat, dir_count):
    width = table.shape[3]
    flat_table = table.reshape(2, NT0 * dir_count, width)
    leaf_product = jnp.einsum(
        "cqu,udrb->cdrqb", flat_table, source_flat, preferred_element_type=jnp.float32
    )
    leaf = jnp.stack(
        [leaf_product[0, 0] - leaf_product[1, 1], leaf_product[0, 1] + leaf_product[1, 0]]
    )
    return leaf.reshape((2, source_flat.shape[2], NT0, dir_count, source_flat.shape[3]))


def shards(
    source,
    near_blocks,
    near_mask,
    radiate,
    receive,
    theta_one,
    theta_two,
    theta_three,
    phi_taps,
    shift_one,
    shift_two,
    shift_three,
    trans_one,
    trans_two,
    trans_three,
    far_lists,
):
    width = source.shape[0]
    rhs_count = source.shape[2]
    layers = source.shape[3]
    plane_size = source.shape[4]
    boxes = layers * plane_size
    own_rows = near_blocks.shape[2]
    rimmed = padded_2(source, (("box", 3),), 1, False)
    margin = GZ + 1
    flat_rim = rimmed.reshape(width, 2, rhs_count, (layers + 2) * plane_size)
    flat_rim = jnp.pad(flat_rim, ((0, 0),) * 3 + ((margin, margin),))
    leaf_index = np.arange(boxes)
    leaf_y = leaf_index // GZ % GY
    leaf_z = leaf_index % GZ
    mask_float = near_mask.astype(jnp.float32).reshape(near_mask.shape[0], boxes)
    near_total = jnp.zeros((own_rows, 2, rhs_count, boxes), jnp.float32)
    for group_x in range(3):
        products = jnp.einsum(
            "kcvu,udrb->kcdvrb",
            near_blocks[9 * group_x : 9 * group_x + 9],
            flat_rim,
            preferred_element_type=jnp.float32,
        )
        for inner in range(9):
            shift_y = inner // 3 - 1
            shift_z = inner % 3 - 1
            start = margin + group_x * plane_size + shift_y * GZ + shift_z
            piece = products[inner, :, :, :, :, start : start + boxes]
            term = jnp.stack([piece[0, 0] - piece[1, 1], piece[0, 1] + piece[1, 0]], axis=1)
            valid = (
                (leaf_y + shift_y >= 0)
                & (leaf_y + shift_y < GY)
                & (leaf_z + shift_z >= 0)
                & (leaf_z + shift_z < GZ)
            ).astype(np.float32)
            near_total = near_total + mask_float[9 * group_x + inner] * jnp.asarray(valid) * term
    dirs_local = radiate.shape[2]
    source_flat = source.reshape(width, 2, rhs_count, boxes)
    leaf = leaf_pattern(radiate, source_flat, dirs_local)
    first = phi_up(leaf, phi_taps[0])
    plane_one = plane_size // 4
    row_one = GZ // 2
    layers_one = layers // 2
    group = 1
    while group * plane_size < 512 and 2 * group <= layers_one:
        group = 2 * group
    block = jnp.asarray(block_table(plane_size, GZ, group))
    cos_one, sin_one = phase_tables(shift_one, layers, GY, GZ)
    moved = turn_phase(theta_boxes(theta_one, first), cos_one, sin_one, 1.0)
    grouped = moved.reshape(moved.shape[:4] + (layers_one // group, 2 * group * plane_size))
    level_one = jnp.einsum("crtpan,nm->crtpam", grouped, block, precision=HIGHEST)
    level_one = level_one.reshape(moved.shape[:4] + (boxes // 8,))
    parent = jnp.asarray(parent_table(layers_one, GY // 2, GZ // 2))
    cos_two, sin_two = phase_tables(shift_two, layers_one, GY // 2, GZ // 2)
    moved = turn_phase(
        theta_boxes(theta_two, phi_up(level_one, phi_taps[1])), cos_two, sin_two, 1.0
    )
    level_two = jnp.einsum("crtpb,bm->crmpt", moved, parent, precision=HIGHEST)
    moved = theta_upper(theta_three, phi_up(level_two, phi_taps[2]))
    dirs_top = moved.shape[3] * moved.shape[4]
    layers_top = layers // 8
    split_top = moved.reshape((2, rhs_count, layers_top, 2, GY // 8, 2, GZ // 8, 2, dirs_top))
    angles_top = jnp.transpose(shift_three, (0, 2, 1)).reshape(2, 2, 2, dirs_top)
    cos_top = jnp.cos(angles_top)
    sin_top = jnp.sin(angles_top)
    form = "raxbyezq,xyzq->rabeq"
    top_real = jnp.einsum(form, split_top[0], cos_top, precision=HIGHEST) - jnp.einsum(
        form, split_top[1], sin_top, precision=HIGHEST
    )
    top_imag = jnp.einsum(form, split_top[1], cos_top, precision=HIGHEST) + jnp.einsum(
        form, split_top[0], sin_top, precision=HIGHEST
    )
    top = jnp.stack([top_real, top_imag])
    extended_one = padded_2(level_one, (("box", 4),), 2 * plane_one, False)
    field_one = translate_flat(extended_one, trans_one, far_lists[0], plane_one, row_one)
    dirs_two = level_two.shape[3] * level_two.shape[4]
    upper = level_two.reshape((2, rhs_count, layers // 4, GY // 4, GZ // 4, dirs_two))
    extended_two = padded_2(upper, (("box", 2),), 2, False)
    count_k = trans_two.shape[0]
    table_two = jnp.transpose(trans_two, (0, 1, 3, 2)).reshape(count_k, 2, dirs_two)
    field_two = translate_upper(extended_two, table_two, far_lists[1]).reshape(level_two.shape)
    table_three = jnp.transpose(trans_three, (0, 1, 3, 2)).reshape(count_k, 2, dirs_top)
    block_dirs = dirs_top // lax.axis_size("box")
    table_block = lax.dynamic_slice_in_dim(
        table_three, lax.axis_index("box") * block_dirs, block_dirs, 2
    )
    extended = jnp.pad(
        lax.all_to_all(top, "box", split_axis=5, concat_axis=2, tiled=True),
        ((0, 0),) * 2 + ((2, 2),) + ((0, 0),) * 3,
    )
    local_field = translate_upper(extended, table_block, far_lists[2])
    top_field = lax.all_to_all(local_field, "box", split_axis=2, concat_axis=5, tiled=True)
    cos_wide = cos_top.reshape(1, 1, 2, 1, 2, 1, 2, dirs_top)
    sin_wide = sin_top.reshape(1, 1, 2, 1, 2, 1, 2, dirs_top)
    field_real = top_field[0][:, :, None, :, None, :, None, :]
    field_imag = top_field[1][:, :, None, :, None, :, None, :]
    spread_real = (field_real * cos_wide + field_imag * sin_wide).reshape(moved.shape[1:])
    spread_imag = (field_imag * cos_wide - field_real * sin_wide).reshape(moved.shape[1:])
    spread = jnp.stack([spread_real, spread_imag])
    spread = phi_down(theta_upper_back(theta_three, spread), phi_taps[2])
    incoming_two = field_two + spread
    spread = jnp.einsum("crmpt,bm->crtpb", incoming_two, parent, precision=HIGHEST)
    spread = turn_phase(spread, cos_two, sin_two, -1.0)
    spread = phi_down(theta_boxes_back(theta_two, spread), phi_taps[1])
    incoming_one = field_one + spread
    grouped = incoming_one.reshape(
        incoming_one.shape[:4] + (layers_one // group, group * plane_one)
    )
    spread = jnp.einsum("crtpam,nm->crtpan", grouped, block, precision=HIGHEST)
    spread = spread.reshape(incoming_one.shape[:4] + (boxes,))
    spread = turn_phase(spread, cos_one, sin_one, -1.0)
    incoming = phi_down(theta_boxes_back(theta_one, spread), phi_taps[0])
    receive_float = receive.astype(jnp.float32)
    far = complex_rows(receive_float, lax.all_gather(incoming, "dir", axis=3, tiled=True))
    return (near_total + far).reshape(own_rows, 2, rhs_count, layers, plane_size)


def solution(mesh):
    placed = (
        P(None, None, None, "box", None),
        P(None, None, "dir", None),
        P(None, "box", None),
        P(None, None, "dir", None),
        P(None, None, None, "dir"),
        P(),
        P(),
        P(),
        P(),
        P(None, None, "dir"),
        P(None, None, "dir"),
        P(None, None, "dir"),
        P(None, None, None, "dir"),
        P(None, None, None, "dir"),
        P(None, None, None, "dir"),
        P(),
    )
    return jax.shard_map(
        shards,
        mesh=mesh,
        in_specs=placed,
        out_specs=P("dir", None, None, "box", None),
        check_vma=False,
    )
```

profile of v0, /device:TPU:1, one launch (start us, length us, event | category | flops | bytes accessed | tf_op | source)
XLA Modules:
  0.0 547.9 jit_solution(1479112081623519294)
XLA Ops:
  6.6 1.2 reshape.1747
  7.8 0.9 convolution_bitcast_fusion.5
  9.0 17.0 %collective-permute-start.2 = (f32[2,2,8,1,1024]{4,2,1,0,3:T(8,128)S(1)}, f32[2,2,8,1,1024]{4,2,1,0,3:T(8,128)S(1)}, u32[]{:S(2)}, u32[]{:S(2)}) collective-permute-start(f32[2,2,8,1,1024]{4,2,1,0,3:T(8,128)S(1)} %maximum_bitcast_fusion), channel_id=1, source_target_pairs={{0,1},{1,2},{2,3},{3,4},{4,5},{5,6},{6,7},{7,8},{8,9},{9,10},{10,1... | collective-permute-start | bytes 393224 | tf_op jit(solution)/shard_map/ppermute | solution.py:23
  25.9 1.9 collective-permute-start.3
  28.1 3.2 collective-permute-start
  31.3 1.3 collective-permute-start.1
  32.6 1.4 broadcast_multiply_fusion.4
  35.2 1.1 broadcast_multiply_fusion.8
  36.4 0.9 cosine_bitcast_fusion.1
  39.4 1.1 copy.518
  49.8 3.4 fusion.176
  54.5 2.5 fusion.177
  69.9 3.5 fusion.178
  80.4 12.6 %collective-permute-start.6 = (f32[2,2,16,1,128]{4,2,3,1,0:T(8,128)S(1)}, f32[2,2,16,1,128]{4,2,3,1,0:T(8,128)S(1)}, u32[]{:S(2)}, u32[]{:S(2)}) collective-permute-start(f32[2,2,16,1,128]{4,2,3,1,0:T(8,128)S(1)} %get-tuple-element.198), channel_id=1, source_target_pairs={{0,1},{1,2},{2,3},{3,4},{4,5},{5,6},{6,7},{7,8},{8,9},{9,10},{10,1... | collective-permute-start | bytes 98312 | tf_op jit(solution)/shard_map/ppermute | solution.py:23
  93.1 1.9 collective-permute-start.7
  95.1 4.3 collective-permute-start.4
  99.4 1.3 collective-permute-start.5
  100.7 6.4 %collective-permute-done.7 = f32[2,2,16,1,128]{4,2,3,1,0:T(8,128)S(1)} collective-permute-done((f32[2,2,16,1,128]{4,2,3,1,0:T(8,128)S(1)}, f32[2,2,16,1,128]{4,2,3,1,0:T(8,128)S(1)}, u32[]{:S(2)}, u32[]{:S(2)}) %collective-permute-start.7) | collective-permute-done | bytes 32800 | tf_op jit(solution)/shard_map/ppermute | solution.py:25
  107.6 1.1 convolution_bitcast_fusion.8
  108.9 4.9 collective-permute-start.8
  113.8 1.3 collective-permute-start.9
  115.1 6.6 %collective-permute-start.10 = (f32[2,2,16,1,32]{4,2,3,1,0:T(8,128)S(1)}, f32[2,2,16,1,32]{4,2,3,1,0:T(8,128)S(1)}, u32[]{:S(2)}, u32[]{:S(2)}) collective-permute-start(f32[2,2,16,1,32]{4,2,3,1,0:T(8,128)S(1)} %get-tuple-element.145), channel_id=1, source_target_pairs={{0,1},{1,2},{2,3},{3,4},{4,5},{5,6},{6,7},{7,8},{8,9},{9,10},{10,1... | collective-permute-start | bytes 24584 | tf_op jit(solution)/shard_map/ppermute | solution.py:23
  121.7 1.9 collective-permute-start.11
  124.9 19.7 %gather_fusion = f32[32,2,2,16,2,128]{3,4,2,1,5,0:T(2,128)} fusion(f32[2,2,16,2,292]{2,3,1,0,4:T(2,128)S(1)} %pad.22.clone, s32[32]{0:T(128)S(1)} %get-tuple-element.213), kind=kCustom, calls=%fused_computation | custom fusion | bytes 4194944 | tf_op jit(solution)/shard_map/vmap()/gather | solution.py:145
  144.6 11.9 %broadcast_multiply_fusion = f32[32,2,2,16,2,128]{3,4,2,1,5,0:T(2,128)} fusion(f32[32,2,2,16,2,128]{3,4,2,1,5,0:T(2,128)} %gather_fusion, f32[32,128]{1,0:T(8,128)S(1)} %copy-done.61), kind=kLoop, calls=%fused_computation.3 | loop fusion | flops 524288 | bytes 4210688 | tf_op jit(solution)/shard_map/vmap()/mul | solution.py:149
  156.5 13.2 %copy.499 = f32[32,2,2,16,2,128]{5,0,2,1,4,3:T(8,128)S(1)} copy(f32[32,2,2,16,2,128]{3,4,2,1,5,0:T(2,128)} %broadcast_multiply_fusion) | data formatting | bytes 4194304 | tf_op jit(solution)/shard_map/vmap()/mul | solution.py:149
  169.8 1.2 fusion.104
  173.6 2.0 reshape.1907
  175.6 14.7 %all-to-all-start = ((f32[32,1,128]{2,1,0:T(1,128)}), f32[32,1,128]{2,1,0:T(1,128)S(1)}, u32[]{:S(2)}, u32[]{:S(2)}) async-start(f32[32,1,128]{2,1,0:T(1,128)} %reshape.1907), calls=%async_computation | async-start | bytes 32768 | tf_op jit(solution)/shard_map/all_to_all | solution.py:297
  190.3 1.0 select_maximum_fusion
  191.4 1.8 gather_fusion.1
  193.1 3.7 copy.507
  196.8 4.9 all-to-all-done
  203.1 1.6 reshape.1908
  204.7 1.0 copy.517
  206.3 7.8 %gather_fusion.2 = f32[32,2,2,32,2,16]{5,2,1,4,3,0:T(2,128)} fusion(f32[2,2,36,5,6,16]{5,1,0,3,4,2:T(2,128)S(1)} %pad.148, s32[32]{0:T(128)S(1)} %or_bitcast_fusion), kind=kCustom, calls=%fused_computation.2 | custom fusion | bytes 1049344 | tf_op jit(solution)/shard_map/vmap()/gather | solution.py:163
  214.1 5.6 %copy.519 = f32[32,2,2,32,2,16]{3,0,4,2,1,5:T(8,128)S(1)} copy(f32[32,2,2,32,2,16]{5,2,1,4,3,0:T(2,128)} %gather_fusion.2) | data formatting | bytes 1048576 | tf_op jit(solution)/shard_map/vmap()/gather | solution.py:163
  219.7 2.0 convolution_bitcast_fusion.9
  222.0 0.8 reshape.1909
  222.8 7.2 %all-to-all-start.1 = ((f32[32,1,128]{2,1,0:T(1,128)}), f32[32,1,128]{2,1,0:T(1,128)S(1)}, u32[]{:S(2)}, u32[]{:S(2)}) async-start(f32[32,1,128]{2,1,0:T(1,128)} %reshape.1909), calls=%async_computation.1 | async-start | bytes 32768 | tf_op jit(solution)/shard_map/all_to_all | solution.py:301
  230.1 112.5 %convolution_bitcast_fusion.3 = f32[2,2,2,2,2,4,128]{5,0,4,3,2,1,6:T(2,128)S(1)} fusion(f32[32,2,2,2,2,4,128]{0,5,4,3,2,1,6:T(4,128)} %copy.507, f32[32,2,128,1,1,1,1]{0,1,6,5,4,3,2:T(2,128)S(1)} %bitcast.547), kind=kOutput, calls=%fused_computation.7 | convolution fusion | flops 6291456 | bytes 1146880 | tf_op jit(solution)/shard_map/kcq,kdrxyzq->cdrxyzq/dot_general | solution.py:166
  344.3 1.1 broadcast_multiply_fusion.3
  345.4 1.0 reduce_sum.94
  347.1 11.3 %collective-permute-start.12 = (f32[6,2,16,1,32]{4,2,3,1,0:T(8,128)}, f32[6,2,16,1,32]{4,2,3,1,0:T(8,128)}, u32[]{:S(2)}, u32[]{:S(2)}) collective-permute-start(f32[6,2,16,1,32]{4,2,3,1,0:T(8,128)} %get-tuple-element.68), channel_id=1, source_target_pairs={{1,0},{2,1},{3,2},{4,3},{5,4},{6,5},{7,6},{8,7},{9,8},{10,9},{11,1... | collective-permute-start | bytes 73736 | tf_op jit(solution)/shard_map/ppermute | solution.py:25
  358.5 3.8 collective-permute-start.13
  362.3 1.9 slice_subtract_fusion
  364.2 1.2 copy.509
  366.4 1.6 convolution_bitcast_fusion.6
  368.0 0.9 multiply_subtract_fusion.2
  369.4 11.3 %collective-permute-start.14 = (f32[6,2,16,1,128]{4,2,3,1,0:T(8,128)S(1)}, f32[6,2,16,1,128]{4,2,3,1,0:T(8,128)S(1)}, u32[]{:S(2)}, u32[]{:S(2)}) collective-permute-start(f32[6,2,16,1,128]{4,2,3,1,0:T(8,128)S(1)} %get-tuple-element.79), channel_id=1, source_target_pairs={{1,0},{2,1},{3,2},{4,3},{5,4},{6,5},{7,6},{8,7},{9,8},{10,9},{11,1... | collective-permute-start | bytes 294920 | tf_op jit(solution)/shard_map/ppermute | solution.py:25
  380.8 3.9 collective-permute-start.15
  385.0 3.5 collective-permute-done.15
  389.9 13.7 %collective-permute-start.16 = (f32[6,2,8,1,1024]{4,2,1,0,3:T(8,128)S(1)}, f32[6,2,8,1,1024]{4,2,1,0,3:T(8,128)S(1)}, u32[]{:S(2)}, u32[]{:S(2)}) collective-permute-start(f32[6,2,8,1,1024]{4,2,1,0,3:T(8,128)S(1)} %pad_maximum_fusion.2), channel_id=1, source_target_pairs={{1,0},{2,1},{3,2},{4,3},{5,4},{6,5},{7,6},{8,7},{9,8},{10,9},{11,1... | collective-permute-start | bytes 1179656 | tf_op jit(solution)/shard_map/ppermute | solution.py:25
  403.5 1.9 collective-permute-start.17
  405.6 3.4 collective-permute-done.16
  409.0 28.9 %collective-permute-done.17 = f32[6,2,8,1,1024]{4,2,1,0,3:T(8,128)} collective-permute-done((f32[6,2,8,1,1024]{4,2,1,0,3:T(8,128)S(1)}, f32[6,2,8,1,1024]{4,2,1,0,3:T(8,128)}, u32[]{:S(2)}, u32[]{:S(2)}) %collective-permute-start.17) | collective-permute-done | bytes 393248 | tf_op jit(solution)/shard_map/ppermute | solution.py:23
  437.9 1.6 slice_add_fusion.1
  441.5 91.4 %all-gather.2.cloned.1.call-done = f32[2,2,8,16,1024]{4,2,1,0,3:T(8,128)} async-done(((f32[2,2,8,1,1024]{4,2,1,0,3:T(8,128)}), f32[2,2,8,16,1024]{4,2,1,0,3:T(8,128)}) %all-gather.2.cloned.1.call-update) | async-done | bytes 2097168 | tf_op jit(solution)/shard_map/all_gather | solution.py:323
  532.9 1.7 fusion.179
  535.0 1.0 convolution_bitcast_fusion.12
  536.1 1.0 convolution_bitcast_fusion.10
  537.1 1.0 fusion.1
  538.2 1.0 fusion.3
  539.6 1.0 copy_add_fusion
  (492 shorter events, 47.4 us)
Async XLA Ops:
  6.5 163.2 %copy-start = (f32[32,2,16,2]{0,3,2,1:T(2,128)S(1)}, f32[32,2,16,2]{0,3,2,1:T(2,128)}, u32[]{:S(2)}) copy-start(f32[32,2,16,2]{0,3,2,1:T(2,128)} %param.59) | copy-start | bytes 24580
  6.5 28.7 %copy-start.114 = (f32[8,128,1]{1,0,2:T(8,128)S(1)}, f32[8,128,1]{1,0,2:T(8,128)}, u32[]{:S(2)}) copy-start(f32[8,128,1]{1,0,2:T(8,128)} %constant.309) | copy-start | bytes 12292
  6.6 28.7 %copy-start.97 = (f32[8,32,4]{1,2,0:T(4,128)S(1)}, f32[8,32,4]{1,2,0:T(4,128)}, u32[]{:S(2)}) copy-start(f32[8,32,4]{1,2,0:T(4,128)} %param.57) | copy-start | bytes 12292
  6.6 30.6 %copy-start.99 = (s32[3,32,3]{1,2,0:T(4,128)S(1)}, s32[3,32,3]{1,2,0:T(4,128)}, u32[]{:S(2)}) copy-start(s32[3,32,3]{1,2,0:T(4,128)} %param.62) | copy-start | bytes 3460
  6.6 30.7 %copy-start.40 = (f32[32,2,32,4]{2,3,1,0:T(4,128)S(1)}, f32[32,2,32,4]{2,3,1,0:T(4,128)}, u32[]{:S(2)}) copy-start(f32[32,2,32,4]{2,3,1,0:T(4,128)} %param.60) | copy-start | bytes 98308
  6.6 32.4 %copy-start.67 = (f32[8,64,8]{1,2,0:T(8,128)S(1)}, f32[8,64,8]{1,2,0:T(8,128)}, u32[]{:S(2)}) copy-start(f32[8,64,8]{1,2,0:T(8,128)} %param.58) | copy-start | bytes 49156
  6.6 32.8 %copy-start.22 = (f32[32,2,64,8]{2,3,1,0:T(8,128)S(1)}, f32[32,2,64,8]{2,3,1,0:T(8,128)}, u32[]{:S(2)}) copy-start(f32[32,2,64,8]{2,3,1,0:T(8,128)} %param.61) | copy-start | bytes 393220
  8.8 36.9 %copy-start.62 = (bf16[27,2,4,64]{3,2,1,0:T(4,128)(2,1)S(1)}, bf16[27,2,4,64]{3,2,1,0:T(4,128)(2,1)}, u32[]{:S(2)}) copy-start(bf16[27,2,4,64]{3,2,1,0:T(4,128)(2,1)} %param.48) | copy-start | bytes 82948
  8.8 37.0 %copy-start.57 = (s32[27,8,128]{2,1,0:T(8,128)S(1)}, s32[27,8,128]{2,1,0:T(8,128)}, u32[]{:S(2)}) copy-start(s32[27,8,128]{2,1,0:T(8,128)} %param.49) | copy-start | bytes 331780
  8.8 37.6 %copy-start.110 = (f32[1,8,128]{2,1,0:T(8,128)S(1)}, f32[1,8,128]{2,1,0:T(8,128)}, u32[]{:S(2)}) copy-start(f32[1,8,128]{2,1,0:T(8,128)} %constant.149) | copy-start | bytes 12292
  8.8 37.6 %copy-start.111 = (f32[1,8,128]{2,1,0:T(8,128)S(1)}, f32[1,8,128]{2,1,0:T(8,128)}, u32[]{:S(2)}) copy-start(f32[1,8,128]{2,1,0:T(8,128)} %constant.154) | copy-start | bytes 12292
  8.9 37.6 %copy-start.112 = (f32[1,8,128]{2,1,0:T(8,128)S(1)}, f32[1,8,128]{2,1,0:T(8,128)}, u32[]{:S(2)}) copy-start(f32[1,8,128]{2,1,0:T(8,128)} %constant.155) | copy-start | bytes 12292
  8.9 37.6 %copy-start.113 = (f32[1,8,128]{2,1,0:T(8,128)S(1)}, f32[1,8,128]{2,1,0:T(8,128)}, u32[]{:S(2)}) copy-start(f32[1,8,128]{2,1,0:T(8,128)} %constant.156) | copy-start | bytes 12292
  8.9 38.3 %copy-start.106 = (f32[1,8,128]{2,1,0:T(8,128)S(1)}, f32[1,8,128]{2,1,0:T(8,128)}, u32[]{:S(2)}) copy-start(f32[1,8,128]{2,1,0:T(8,128)} %constant.150) | copy-start | bytes 12292
  8.9 38.3 %copy-start.107 = (f32[1,8,128]{2,1,0:T(8,128)S(1)}, f32[1,8,128]{2,1,0:T(8,128)}, u32[]{:S(2)}) copy-start(f32[1,8,128]{2,1,0:T(8,128)} %constant.151) | copy-start | bytes 12292
  8.9 38.3 %copy-start.108 = (f32[1,8,128]{2,1,0:T(8,128)S(1)}, f32[1,8,128]{2,1,0:T(8,128)}, u32[]{:S(2)}) copy-start(f32[1,8,128]{2,1,0:T(8,128)} %constant.152) | copy-start | bytes 12292
  8.9 38.3 %copy-start.109 = (f32[1,8,128]{2,1,0:T(8,128)S(1)}, f32[1,8,128]{2,1,0:T(8,128)}, u32[]{:S(2)}) copy-start(f32[1,8,128]{2,1,0:T(8,128)} %constant.153) | copy-start | bytes 12292
  9.0 69.7 %collective-permute-start.2 = (f32[2,2,8,1,1024]{4,2,1,0,3:T(8,128)S(1)}, f32[2,2,8,1,1024]{4,2,1,0,3:T(8,128)S(1)}, u32[]{:S(2)}, u32[]{:S(2)}) collective-permute-start(f32[2,2,8,1,1024]{4,2,1,0,3:T(8,128)S(1)} %maximum_bitcast_fusion), channel_id=1, source_target_pairs={{0,1},{1,2},{2,3},{3,4},{4,5},{5,6},{6,7},{7,8},{8,9},{9,10},{10,1... | collective-permute-start | bytes 393224 | tf_op jit(solution)/shard_map/ppermute | solution.py:23
  25.9 52.7 %collective-permute-start.3 = (f32[2,2,8,1,1024]{4,2,1,0,3:T(8,128)S(1)}, f32[2,2,8,1,1024]{4,2,1,0,3:T(8,128)S(1)}, u32[]{:S(2)}, u32[]{:S(2)}) collective-permute-start(f32[2,2,8,1,1024]{4,2,1,0,3:T(8,128)S(1)} %maximum_bitcast_fusion), channel_id=1, source_target_pairs={{1,0},{2,1},{3,2},{4,3},{5,4},{6,5},{7,6},{8,7},{9,8},{10,9},{11,1... | collective-permute-start | bytes 393224 | tf_op jit(solution)/shard_map/ppermute | solution.py:25
  28.1 20.0 %collective-permute-start = (bf16[64,2,2,1,128]{4,3,2,1,0:T(2,128)(2,1)S(1)}, bf16[64,2,2,1,128]{4,3,2,1,0:T(2,128)(2,1)S(1)}, u32[]{:S(2)}, u32[]{:S(2)}) collective-permute-start(bf16[64,2,2,1,128]{4,3,2,1,0:T(2,128)(2,1)S(1)} %get-tuple-element.64), channel_id=1, source_target_pairs={{0,16},{16,32},{32,48},{48,64},{64,80},{80,96},{96,112},{112,128},... | collective-permute-start | bytes 196616 | tf_op jit(solution)/shard_map/ppermute | solution.py:23
  31.3 16.8 %collective-permute-start.1 = (bf16[64,2,2,1,128]{4,3,2,1,0:T(2,128)(2,1)S(1)}, bf16[64,2,2,1,128]{4,3,2,1,0:T(2,128)(2,1)S(1)}, u32[]{:S(2)}, u32[]{:S(2)}) collective-permute-start(bf16[64,2,2,1,128]{4,3,2,1,0:T(2,128)(2,1)S(1)} %get-tuple-element.65), channel_id=1, source_target_pairs={{16,0},{32,16},{48,32},{64,48},{80,64},{96,80},{112,96},{128,112},... | collective-permute-start | bytes 196616 | tf_op jit(solution)/shard_map/ppermute | solution.py:25
  48.0 30.9 %copy-start.100 = (f32[2]{0:T(128)}, f32[2]{0:T(128)S(1)}, u32[]{:S(2)}) copy-start(f32[2]{0:T(128)S(1)} %get-tuple-element.26) | copy-start | bytes 28
  48.0 30.9 %copy-start.102 = (f32[2]{0:T(128)}, f32[2]{0:T(128)S(1)}, u32[]{:S(2)}) copy-start(f32[2]{0:T(128)S(1)} %get-tuple-element.27) | copy-start | bytes 28
  48.0 30.9 %copy-start.104 = (f32[2]{0:T(128)}, f32[2]{0:T(128)S(1)}, u32[]{:S(2)}) copy-start(f32[2]{0:T(128)S(1)} %get-tuple-element.28) | copy-start | bytes 28
  78.9 28.2 %copy-start.63 = (f32[32,16]{0,1:T(8,128)S(1)}, f32[32,16]{0,1:T(8,128)}, u32[]{:S(2)}) copy-start(f32[32,16]{0,1:T(8,128)} %param.53) | copy-start | bytes 6148
  78.9 28.6 %copy-start.23 = (f32[32,4,128]{2,0,1:T(8,128)S(1)}, f32[32,4,128]{2,0,1:T(8,128)}, u32[]{:S(2)}) copy-start(f32[32,4,128]{2,0,1:T(8,128)} %get-tuple-element.197) | copy-start | bytes 196612
  80.4 20.2 %collective-permute-start.6 = (f32[2,2,16,1,128]{4,2,3,1,0:T(8,128)S(1)}, f32[2,2,16,1,128]{4,2,3,1,0:T(8,128)S(1)}, u32[]{:S(2)}, u32[]{:S(2)}) collective-permute-start(f32[2,2,16,1,128]{4,2,3,1,0:T(8,128)S(1)} %get-tuple-element.198), channel_id=1, source_target_pairs={{0,1},{1,2},{2,3},{3,4},{4,5},{5,6},{6,7},{7,8},{8,9},{9,10},{10,1... | collective-permute-start | bytes 98312 | tf_op jit(solution)/shard_map/ppermute | solution.py:23
  93.1 13.9 %collective-permute-start.7 = (f32[2,2,16,1,128]{4,2,3,1,0:T(8,128)S(1)}, f32[2,2,16,1,128]{4,2,3,1,0:T(8,128)S(1)}, u32[]{:S(2)}, u32[]{:S(2)}) collective-permute-start(f32[2,2,16,1,128]{4,2,3,1,0:T(8,128)S(1)} %get-tuple-element.199), channel_id=1, source_target_pairs={{1,0},{2,1},{3,2},{4,3},{5,4},{6,5},{7,6},{8,7},{9,8},{10,9},{11,1... | collective-permute-start | bytes 98312 | tf_op jit(solution)/shard_map/ppermute | solution.py:25
  95.1 26.6 %collective-permute-start.4 = (f32[2,2,16,2,64]{4,2,3,1,0:T(8,128)S(1)}, f32[2,2,16,2,64]{4,2,3,1,0:T(8,128)S(1)}, u32[]{:S(2)}, u32[]{:S(2)}) collective-permute-start(f32[2,2,16,2,64]{4,2,3,1,0:T(8,128)S(1)} %get-tuple-element.194), channel_id=1, source_target_pairs={{0,16},{16,32},{32,48},{48,64},{64,80},{80,96},{96,112},{112,128},... | collective-permute-start | bytes 98312 | tf_op jit(solution)/shard_map/ppermute | solution.py:23
  99.4 24.3 %collective-permute-start.5 = (f32[2,2,16,2,64]{4,2,3,1,0:T(8,128)S(1)}, f32[2,2,16,2,64]{4,2,3,1,0:T(8,128)S(1)}, u32[]{:S(2)}, u32[]{:S(2)}) collective-permute-start(f32[2,2,16,2,64]{4,2,3,1,0:T(8,128)S(1)} %get-tuple-element.195), channel_id=1, source_target_pairs={{16,0},{32,16},{48,32},{64,48},{80,64},{96,80},{112,96},{128,112},... | collective-permute-start | bytes 98312 | tf_op jit(solution)/shard_map/ppermute | solution.py:25
  108.9 81.4 %collective-permute-start.8 = (f32[2,2,2,2,4,128]{5,1,0,4,3,2:T(2,128)S(1)}, f32[2,2,2,2,4,128]{5,1,0,4,3,2:T(2,128)}, u32[]{:S(2)}, u32[]{:S(2)}) collective-permute-start(f32[2,2,2,2,4,128]{5,1,0,4,3,2:T(2,128)S(1)} %reshape.1891), channel_id=1, source_target_pairs={{0,16},{16,32},{32,48},{48,64},{64,80},{80,96},{96,112},{112,128},... | collective-permute-start | bytes 98312 | tf_op jit(solution)/shard_map/ppermute | solution.py:23
  113.8 76.5 %collective-permute-start.9 = (f32[2,2,2,2,4,128]{5,1,0,4,3,2:T(2,128)S(1)}, f32[2,2,2,2,4,128]{5,1,0,4,3,2:T(2,128)}, u32[]{:S(2)}, u32[]{:S(2)}) collective-permute-start(f32[2,2,2,2,4,128]{5,1,0,4,3,2:T(2,128)S(1)} %reshape.1891), channel_id=1, source_target_pairs={{16,0},{32,16},{48,32},{64,48},{80,64},{96,80},{112,96},{128,112},... | collective-permute-start | bytes 98312 | tf_op jit(solution)/shard_map/ppermute | solution.py:25
  115.1 56.6 %collective-permute-start.10 = (f32[2,2,16,1,32]{4,2,3,1,0:T(8,128)S(1)}, f32[2,2,16,1,32]{4,2,3,1,0:T(8,128)S(1)}, u32[]{:S(2)}, u32[]{:S(2)}) collective-permute-start(f32[2,2,16,1,32]{4,2,3,1,0:T(8,128)S(1)} %get-tuple-element.145), channel_id=1, source_target_pairs={{0,1},{1,2},{2,3},{3,4},{4,5},{5,6},{6,7},{7,8},{8,9},{9,10},{10,1... | collective-permute-start | bytes 24584 | tf_op jit(solution)/shard_map/ppermute | solution.py:23
  121.7 50.1 %collective-permute-start.11 = (f32[2,2,16,1,32]{4,2,3,1,0:T(8,128)S(1)}, f32[2,2,16,1,32]{4,2,3,1,0:T(8,128)S(1)}, u32[]{:S(2)}, u32[]{:S(2)}) collective-permute-start(f32[2,2,16,1,32]{4,2,3,1,0:T(8,128)S(1)} %get-tuple-element.146), channel_id=1, source_target_pairs={{1,0},{2,1},{3,2},{4,3},{5,4},{6,5},{7,6},{8,7},{9,8},{10,9},{11,1... | collective-permute-start | bytes 24584 | tf_op jit(solution)/shard_map/ppermute | solution.py:25
  175.6 26.2 %all-to-all-start = ((f32[32,1,128]{2,1,0:T(1,128)}), f32[32,1,128]{2,1,0:T(1,128)S(1)}, u32[]{:S(2)}, u32[]{:S(2)}) async-start(f32[32,1,128]{2,1,0:T(1,128)} %reshape.1907), calls=%async_computation | async-start | bytes 32768 | tf_op jit(solution)/shard_map/all_to_all | solution.py:297
  222.8 119.8 %all-to-all-start.1 = ((f32[32,1,128]{2,1,0:T(1,128)}), f32[32,1,128]{2,1,0:T(1,128)S(1)}, u32[]{:S(2)}, u32[]{:S(2)}) async-start(f32[32,1,128]{2,1,0:T(1,128)} %reshape.1909), calls=%async_computation.1 | async-start | bytes 32768 | tf_op jit(solution)/shard_map/all_to_all | solution.py:301
  230.0 302.9 %all-gather.2.cloned.1.call-start = ((), (), s32[]{:S(2)}) async-start(), calls=%async_computation.2 | async-start | bytes 2228224 | tf_op jit(solution)/shard_map/all_gather | solution.py:323
  230.1 114.1 %copy-start.24 = (f32[16,8,64]{2,0,1:T(8,128)S(1)}, f32[16,8,64]{2,0,1:T(8,128)}, u32[]{:S(2)}) copy-start(f32[16,8,64]{2,0,1:T(8,128)} %copy.524) | copy-start | bytes 98308
  230.1 114.1 %copy-start.25 = (f32[16,8,64]{2,0,1:T(8,128)S(1)}, f32[16,8,64]{2,0,1:T(8,128)}, u32[]{:S(2)}) copy-start(f32[16,8,64]{2,0,1:T(8,128)} %copy.527) | copy-start | bytes 98308
  347.1 18.9 %collective-permute-start.12 = (f32[6,2,16,1,32]{4,2,3,1,0:T(8,128)}, f32[6,2,16,1,32]{4,2,3,1,0:T(8,128)}, u32[]{:S(2)}, u32[]{:S(2)}) collective-permute-start(f32[6,2,16,1,32]{4,2,3,1,0:T(8,128)} %get-tuple-element.68), channel_id=1, source_target_pairs={{1,0},{2,1},{3,2},{4,3},{5,4},{6,5},{7,6},{8,7},{9,8},{10,9},{11,1... | collective-permute-start | bytes 73736 | tf_op jit(solution)/shard_map/ppermute | solution.py:25
  358.5 7.9 %collective-permute-start.13 = (f32[6,2,16,1,32]{4,2,3,1,0:T(8,128)}, f32[6,2,16,1,32]{4,2,3,1,0:T(8,128)}, u32[]{:S(2)}, u32[]{:S(2)}) collective-permute-start(f32[6,2,16,1,32]{4,2,3,1,0:T(8,128)} %get-tuple-element.69), channel_id=1, source_target_pairs={{0,1},{1,2},{2,3},{3,4},{4,5},{5,6},{6,7},{7,8},{8,9},{9,10},{10,1... | collective-permute-start | bytes 73736 | tf_op jit(solution)/shard_map/ppermute | solution.py:23
  369.4 15.6 %collective-permute-start.14 = (f32[6,2,16,1,128]{4,2,3,1,0:T(8,128)S(1)}, f32[6,2,16,1,128]{4,2,3,1,0:T(8,128)S(1)}, u32[]{:S(2)}, u32[]{:S(2)}) collective-permute-start(f32[6,2,16,1,128]{4,2,3,1,0:T(8,128)S(1)} %get-tuple-element.79), channel_id=1, source_target_pairs={{1,0},{2,1},{3,2},{4,3},{5,4},{6,5},{7,6},{8,7},{9,8},{10,9},{11,1... | collective-permute-start | bytes 294920 | tf_op jit(solution)/shard_map/ppermute | solution.py:25
  380.8 7.8 %collective-permute-start.15 = (f32[6,2,16,1,128]{4,2,3,1,0:T(8,128)S(1)}, f32[6,2,16,1,128]{4,2,3,1,0:T(8,128)S(1)}, u32[]{:S(2)}, u32[]{:S(2)}) collective-permute-start(f32[6,2,16,1,128]{4,2,3,1,0:T(8,128)S(1)} %get-tuple-element.80), channel_id=1, source_target_pairs={{0,1},{1,2},{2,3},{3,4},{4,5},{5,6},{6,7},{7,8},{8,9},{9,10},{10,1... | collective-permute-start | bytes 294920 | tf_op jit(solution)/shard_map/ppermute | solution.py:23
  389.1 50.5 %copy-start.17 = (f32[1,2,2,4,2,1024]{5,0,3,1,4,2:T(1,128)S(1)}, f32[1,2,2,4,2,1024]{5,0,3,1,4,2:T(1,128)}, u32[]{:S(2)}) copy-start(f32[1,2,2,4,2,1024]{5,0,3,1,4,2:T(1,128)} %get-tuple-element.48) | copy-start | bytes 393220
  389.1 50.5 %copy-start.18 = (f32[1,2,2,4,2,1024]{5,0,3,1,4,2:T(1,128)S(1)}, f32[1,2,2,4,2,1024]{5,0,3,1,4,2:T(1,128)}, u32[]{:S(2)}) copy-start(f32[1,2,2,4,2,1024]{5,0,3,1,4,2:T(1,128)} %get-tuple-element.49) | copy-start | bytes 393220
  389.2 50.5 %copy-start.41 = (f32[1,1,4,2,1024]{4,2,0,3,1:T(4,128)S(1)}, f32[1,1,4,2,1024]{4,2,0,3,1:T(4,128)}, u32[]{:S(2)}) copy-start(f32[1,1,4,2,1024]{4,2,0,3,1:T(4,128)} %get-tuple-element.101) | copy-start | bytes 98308
  389.3 50.6 %copy-start.42 = (f32[1,1,4,2,1024]{4,2,0,3,1:T(4,128)S(1)}, f32[1,1,4,2,1024]{4,2,0,3,1:T(4,128)}, u32[]{:S(2)}) copy-start(f32[1,1,4,2,1024]{4,2,0,3,1:T(4,128)} %get-tuple-element.103) | copy-start | bytes 98308
  389.3 50.6 %copy-start.43 = (f32[1,1,4,2,1024]{4,2,0,3,1:T(4,128)S(1)}, f32[1,1,4,2,1024]{4,2,0,3,1:T(4,128)}, u32[]{:S(2)}) copy-start(f32[1,1,4,2,1024]{4,2,0,3,1:T(4,128)} %get-tuple-element.105) | copy-start | bytes 98308
  389.3 50.6 %copy-start.44 = (f32[1,1,4,2,1024]{4,2,0,3,1:T(4,128)S(1)}, f32[1,1,4,2,1024]{4,2,0,3,1:T(4,128)}, u32[]{:S(2)}) copy-start(f32[1,1,4,2,1024]{4,2,0,3,1:T(4,128)} %get-tuple-element.107) | copy-start | bytes 98308
  389.3 50.6 %copy-start.45 = (f32[1,1,4,2,1024]{4,2,0,3,1:T(4,128)S(1)}, f32[1,1,4,2,1024]{4,2,0,3,1:T(4,128)}, u32[]{:S(2)}) copy-start(f32[1,1,4,2,1024]{4,2,0,3,1:T(4,128)} %get-tuple-element.109) | copy-start | bytes 98308
  389.3 50.7 %copy-start.46 = (f32[1,1,4,2,1024]{4,2,0,3,1:T(4,128)S(1)}, f32[1,1,4,2,1024]{4,2,0,3,1:T(4,128)}, u32[]{:S(2)}) copy-start(f32[1,1,4,2,1024]{4,2,0,3,1:T(4,128)} %get-tuple-element.111) | copy-start | bytes 98308
  389.7 50.3 %copy-start.47 = (f32[1,1,4,2,1024]{4,2,0,3,1:T(4,128)S(1)}, f32[1,1,4,2,1024]{4,2,0,3,1:T(4,128)}, u32[]{:S(2)}) copy-start(f32[1,1,4,2,1024]{4,2,0,3,1:T(4,128)} %get-tuple-element.113) | copy-start | bytes 98308
  389.7 50.3 %copy-start.48 = (f32[1,1,4,2,1024]{4,2,0,3,1:T(4,128)S(1)}, f32[1,1,4,2,1024]{4,2,0,3,1:T(4,128)}, u32[]{:S(2)}) copy-start(f32[1,1,4,2,1024]{4,2,0,3,1:T(4,128)} %get-tuple-element.115) | copy-start | bytes 98308
  389.8 50.3 %copy-start.49 = (f32[1,1,4,2,1024]{4,2,0,3,1:T(4,128)S(1)}, f32[1,1,4,2,1024]{4,2,0,3,1:T(4,128)}, u32[]{:S(2)}) copy-start(f32[1,1,4,2,1024]{4,2,0,3,1:T(4,128)} %get-tuple-element.119) | copy-start | bytes 98308
  389.8 50.3 %copy-start.50 = (f32[1,1,4,2,1024]{4,2,0,3,1:T(4,128)S(1)}, f32[1,1,4,2,1024]{4,2,0,3,1:T(4,128)}, u32[]{:S(2)}) copy-start(f32[1,1,4,2,1024]{4,2,0,3,1:T(4,128)} %get-tuple-element.121) | copy-start | bytes 98308
  389.8 50.4 %copy-start.51 = (f32[1,1,4,2,1024]{4,2,0,3,1:T(4,128)S(1)}, f32[1,1,4,2,1024]{4,2,0,3,1:T(4,128)}, u32[]{:S(2)}) copy-start(f32[1,1,4,2,1024]{4,2,0,3,1:T(4,128)} %get-tuple-element.123) | copy-start | bytes 98308
  389.8 50.4 %copy-start.52 = (f32[1,1,4,2,1024]{4,2,0,3,1:T(4,128)S(1)}, f32[1,1,4,2,1024]{4,2,0,3,1:T(4,128)}, u32[]{:S(2)}) copy-start(f32[1,1,4,2,1024]{4,2,0,3,1:T(4,128)} %get-tuple-element.125) | copy-start | bytes 98308
  389.8 50.5 %copy-start.15 = (f32[1,2,2,4,2,1024]{5,0,3,1,4,2:T(1,128)S(1)}, f32[1,2,2,4,2,1024]{5,0,3,1,4,2:T(1,128)}, u32[]{:S(2)}) copy-start(f32[1,2,2,4,2,1024]{5,0,3,1,4,2:T(1,128)} %get-tuple-element.30) | copy-start | bytes 393220
  389.8 50.5 %copy-start.16 = (f32[1,2,2,4,2,1024]{5,0,3,1,4,2:T(1,128)S(1)}, f32[1,2,2,4,2,1024]{5,0,3,1,4,2:T(1,128)}, u32[]{:S(2)}) copy-start(f32[1,2,2,4,2,1024]{5,0,3,1,4,2:T(1,128)} %get-tuple-element.31) | copy-start | bytes 393220
  389.9 19.2 %collective-permute-start.16 = (f32[6,2,8,1,1024]{4,2,1,0,3:T(8,128)S(1)}, f32[6,2,8,1,1024]{4,2,1,0,3:T(8,128)S(1)}, u32[]{:S(2)}, u32[]{:S(2)}) collective-permute-start(f32[6,2,8,1,1024]{4,2,1,0,3:T(8,128)S(1)} %pad_maximum_fusion.2), channel_id=1, source_target_pairs={{1,0},{2,1},{3,2},{4,3},{5,4},{6,5},{7,6},{8,7},{9,8},{10,9},{11,1... | collective-permute-start | bytes 1179656 | tf_op jit(solution)/shard_map/ppermute | solution.py:25
  403.5 34.4 %collective-permute-start.17 = (f32[6,2,8,1,1024]{4,2,1,0,3:T(8,128)S(1)}, f32[6,2,8,1,1024]{4,2,1,0,3:T(8,128)}, u32[]{:S(2)}, u32[]{:S(2)}) collective-permute-start(f32[6,2,8,1,1024]{4,2,1,0,3:T(8,128)S(1)} %pad_maximum_fusion.2), channel_id=1, source_target_pairs={{0,1},{1,2},{2,3},{3,4},{4,5},{5,6},{6,7},{7,8},{8,9},{9,10},{10,1... | collective-permute-start | bytes 1179656 | tf_op jit(solution)/shard_map/ppermute | solution.py:23
  405.6 35.0 %copy-start.13 = (f32[1,2,2,4,2,1024]{5,0,3,1,4,2:T(1,128)S(1)}, f32[1,2,2,4,2,1024]{5,0,3,1,4,2:T(1,128)}, u32[]{:S(2)}) copy-start(f32[1,2,2,4,2,1024]{5,0,3,1,4,2:T(1,128)} %get-tuple-element.32) | copy-start | bytes 393220
  405.6 35.0 %copy-start.14 = (f32[1,2,2,4,2,1024]{5,0,3,1,4,2:T(1,128)S(1)}, f32[1,2,2,4,2,1024]{5,0,3,1,4,2:T(1,128)}, u32[]{:S(2)}) copy-start(f32[1,2,2,4,2,1024]{5,0,3,1,4,2:T(1,128)} %get-tuple-element.33) | copy-start | bytes 393220
  441.5 93.1 %copy-start.58 = (bf16[2,8,16,4]{2,3,1,0:T(4,128)(2,1)S(1)}, bf16[2,8,16,4]{2,3,1,0:T(4,128)(2,1)}, u32[]{:S(2)}) copy-start(bf16[2,8,16,4]{2,3,1,0:T(4,128)(2,1)} %param.51) | copy-start | bytes 6148
  (85 other events, 651.3 us)
Sparse Core Ops, SparseCore 0:
  439.6 93.2 all-gather.1
where the time goes:
time: 558 us; the launch traced here: 548 us
  waiting for transfers between devices  139 us (25%)
  matrix products  132 us (24%)
  starting transfers between devices  126 us (23%)
  local copies, waits for them, and re-layouts  100 us (18%)
  other arithmetic  33.1 us (6%)
  between operations  17 us (3%)
    dot_general x2, matrix products, translate_upper(): jnp.einsum('kcq,kdrxyzq->cdrxyzq', table, stacked, precision=HIGHEST)  114 us
    all_gather x1, waiting for transfers between devices, shards(): lax.all_gather(incoming, 'dir', axis=3, tiled=True)  91.4 us
    ppermute x9, starting transfers between devices, padded_2(): lax.ppermute(tail, axis, [(i, (i + 1) % count) for i in range(ends)])  58.1 us
    ppermute x9, starting transfers between devices, padded_2(): lax.ppermute(head, axis, [((i + 1) % count, i) for i in range(ends)])  45.9 us
    ppermute x9, waiting for transfers between devices, padded_2(): lax.ppermute(tail, axis, [(i, (i + 1) % count) for i in range(ends)])  32.8 us
    gather x1, local copies, waits for them, and re-layouts, window(): piece = lax.dynamic_slice_in_dim(padded, start, count, 4)  19.7 us
    gather x4, local copies, waits for them, and re-layouts, window(): return lax.dynamic_slice(padded, start, shape_out)  18.9 us
    all_to_all x1, starting transfers between devices, shards(): lax.all_to_all(top, 'box', split_axis=5, concat_axis=2, tiled=True)  14.7 us
  transfers between devices with their start and end apart: 21, of which 8 were waited for; matrix products, arithmetic and copies ran while one was open for 41% of the time, Pallas kernels for 0%

commit v1 on v0

v1 whole, which is shorter than its diff:
```python
import functools

import jax
import jax.numpy as jnp
import numpy as np
from jax import lax
from jax.experimental import pallas as pl
from jax.experimental.pallas import tpu as pltpu
from jax.sharding import PartitionSpec as P

MESH = pl.DeviceIdType.MESH
F32 = jnp.float32
BF16 = jnp.bfloat16
VMEM_LIMIT = 56 * 1024 * 1024


def iota(shape, dim):
    return lax.broadcasted_iota(jnp.int32, shape, dim)


def split(a):
    high = a.astype(BF16)
    return high, (a - high.astype(F32)).astype(BF16)


def dot(a, b, dims=((1,), (0,))):
    return lax.dot_general(a, b, (dims, ((), ())), preferred_element_type=F32)


def dot3(a, b, dims=((1,), (0,))):
    a_high, a_low = split(a)
    b_high, b_low = split(b)
    return dot(a_high, b_high, dims) + (dot(a_high, b_low, dims) + dot(a_low, b_high, dims))


def dot_left(a, b, dims=((1,), (0,))):
    a_high, a_low = split(a)
    return dot(a_high, b, dims) + dot(a_low, b, dims)


def dot_right(a, b, dims=((1,), (0,))):
    b_high, b_low = split(b)
    return dot(a, b_high, dims) + dot(a, b_low, dims)


def onehot(condition):
    return jnp.where(condition, 1.0, 0.0).astype(BF16)


def interpolation(taps, level, theta, fine, coarse, wide, first, transposed):
    (fine_p, fine_t), (coarse_p, coarse_t) = fine, coarse
    if transposed:
        spread = onehot(iota((fine_t, fine_p * fine_t), 1) % fine_t == iota((fine_t, fine_p * fine_t), 0))
        tiled = jnp.concatenate([dot_left(theta, spread)] * coarse_p, axis=0)
        fine_dim, coarse_dim = 1, 0
    else:
        spread = onehot(
            iota((coarse_t, coarse_p * coarse_t), 1) % coarse_t == iota((coarse_t, coarse_p * coarse_t), 0)
        )
        tiled = jnp.concatenate([dot_left(theta, spread)] * fine_p, axis=0)
        fine_dim, coarse_dim = 0, 1
    p = iota(tiled.shape, fine_dim) // fine_t
    tap = iota(tiled.shape, coarse_dim) // coarse_t - first(p)
    even = wide(p) % 2 == 0
    weight = jnp.zeros(tiled.shape, F32)
    for j in range(3):
        value = jnp.where(even, taps[6 * level + j], taps[6 * level + 3 + j])
        weight = jnp.where(tap == j, value, weight)
    return weight * tiled


def turned(x):
    even = iota(x.shape, 1) % 2 == 0
    count = x.shape[1]
    return jnp.where(even, -pltpu.roll(x, count - 1, 1), pltpu.roll(x, 1, 1))


def child_of_box(index):
    return 4 * (index // 32 % 2) + 2 * (index // 8 % 2) + index % 2


def parent_of_box(index):
    return index // 64 * 8 + index // 16 % 2 * 4 + index // 2 % 4


def upward(
    where, taps, source, shuffle, tables, rims, own_one, own_two, phase_three,
    theta_one, theta_two, theta_two_t, theta_three_t,
    one_ref, two_ref, three_ref, back_two_ref, up_three_ref, phase_two_ref, far_high_ref, far_low_ref,
    leaf, shape_high, shape_low,
):
    me = where[0]
    up_one = interpolation(
        taps, 0, theta_one[...], (6, 16), (5, 8), lambda p: p, lambda p: p // 2, False
    )
    up_two = interpolation(
        taps, 1, theta_two[...], (6, 32), (6, 16), lambda p: p + 1, lambda p: (p + 1) // 2, False
    )
    back_two_ref[...] = interpolation(
        taps, 1, theta_two_t[...], (6, 32), (6, 16), lambda p: p + 1, lambda p: (p + 1) // 2, True
    )
    up_three = interpolation(
        taps, 2, theta_three_t[...], (8, 64), (6, 32), lambda p: p, lambda p: p // 2, True
    )
    up_three_ref[...] = up_three

    gathered = tables[...].astype(F32)
    radiate = jnp.concatenate([gathered[(a - 2) % 16, 8:16] for a in range(5)], axis=0)
    blocks = jnp.concatenate([gathered[e, 0:8] for e in range(16)], axis=0)
    lane = iota((128, 640), 1)
    pick = onehot(iota((128, 640), 0) == lane // 128 * 8 + lane % 8)
    sender = (iota((128, 640), 0) // 8 + me) % 16
    placed = jnp.where(lane % 128 // 8 == sender, dot(blocks.astype(BF16), pick), 0.0)
    summed = placed[0:8]
    for e in range(1, 16):
        summed = summed + placed[8 * e : 8 * e + 8]
    receive = jnp.concatenate([summed[:, 128 * a : 128 * a + 128] for a in range(5)], axis=0)
    send_real = dot_left(up_one, radiate.astype(BF16))
    take_real = dot_left(up_one, receive.astype(BF16))
    send_turned = turned(send_real)
    take_turned = turned(take_real)
    angles = jnp.concatenate([rims[0], own_one[...], rims[1]], axis=0)
    even = iota((96, 128), 1) % 2 == 0
    for o in range(8):
        cosine = angles[:, o : o + 1]
        sine = angles[:, 8 + o : 9 + o]
        moved = cosine * send_real + sine * send_turned
        swapped = jnp.where(even, pltpu.roll(moved, 127, 1), pltpu.roll(moved, 1, 1))
        rows = jnp.concatenate([jnp.where(even, moved, -moved), swapped], axis=0)
        high, low = split(rows)
        shape_high[:, 128 * o : 128 * o + 128] = high
        shape_low[:, 128 * o : 128 * o + 128] = low
        moved = cosine * take_real - sine * take_turned
        columns = jnp.concatenate([moved, turned(moved)], axis=0)
        high, low = split(columns.T)
        far_high_ref[128 * o : 128 * o + 128, :] = high
        far_low_ref[128 * o : 128 * o + 128, :] = low
    for r in range(2):
        for ox in range(2):
            mixed = dot(source[r, ox], shuffle[...]).astype(BF16)
            for o in range(4):
                row = 128 * (4 * ox + o)
                leaf[row : row + 128, 128 * r : 128 * r + 128] = mixed[:, 128 * o : 128 * o + 128]
    level_one = dot(shape_high[...], leaf[...]) + dot(shape_low[...], leaf[...])
    own = jnp.concatenate(
        [level_one[96 * c + 32 : 96 * c + 64, 128 * r : 128 * r + 128] for c in range(2) for r in range(2)],
        axis=0,
    )
    one_ref[...] = own.T

    edges = [pltpu.roll(rims[side], 112, 1) for side in range(2)]
    angles = jnp.concatenate([edges[0], own_two[...], edges[1]], axis=0)
    lane = iota((128, 256), 1)
    kind = child_of_box(lane % 128) + 8 * (lane // 128)
    phases = dot_left(angles, onehot(iota((128, 256), 0) == kind))
    phase_two_ref[...] = phases
    cosine, sine = phases[:, :128], phases[:, 128:]
    parent = onehot(parent_of_box(iota((16, 128), 1)) == iota((16, 128), 0))
    real = dot3(up_two, level_one[:96])
    imag = dot3(up_two, level_one[96:])
    parts = []
    for c in range(2):
        for r in range(2):
            x, y = real[:, 128 * r : 128 * r + 128], imag[:, 128 * r : 128 * r + 128]
            value = x * cosine - y * sine if c == 0 else y * cosine + x * sine
            parts.append(dot_right(parent, value, ((1,), (1,))))
    for index in range(4):
        two_ref[:, 128 * index : 128 * index + 128] = parts[index][:, 32:160]
    level_two = jnp.concatenate(parts, axis=0)
    upper = dot3(level_two, up_three)
    cosine, sine = phase_three[0:16], phase_three[16:32]
    parts = []
    for c in range(2):
        for r in range(2):
            x, y = upper[16 * r : 16 * r + 16], upper[32 + 16 * r : 48 + 16 * r]
            parts.append(x * cosine - y * sine if c == 0 else y * cosine + x * sine)
    row = iota((8, 64), 1)
    together = onehot(row // 16 * 2 + row // 2 % 2 == iota((8, 64), 0))
    three_ref[...] = dot_right(together, jnp.concatenate(parts, axis=0))


def near_part(where, source, halo, blocks, mask, near_ref, products, rolled):
    first, last = where[1] == 0, where[2] == 0
    lane = iota((8, 128), 1)
    for k in range(27):
        dy, dz = k // 3 % 3 - 1, k % 3 - 1
        y, z = lane // 16 + dy, lane % 16 + dz
        valid = (y >= 0) & (y < 8) & (z >= 0) & (z < 16)
        values = jnp.where(valid, mask[k].astype(F32), 0.0)
        rolled[k] = pltpu.roll(values, (16 * dy + dz) % 128, 1)
    for r in range(2):
        for side in range(2):
            edge = dot(blocks[...], halo[side, r])
            products[r, 9 * side] = jnp.where(last if side else first, 0.0, edge)
        for ox in range(2):
            layers = dot(blocks[...], source[r, ox])
            for x in range(4):
                products[r, 1 + 2 * x + ox] = layers[:, 128 * x : 128 * x + 128]
    for r in range(2):
        for x in range(8):
            total = jnp.zeros((8, 128), F32)
            for inner in range(9):
                dy, dz = inner // 3 - 1, inner % 3 - 1
                term = jnp.zeros((8, 128), F32)
                for dx in range(3):
                    k = 9 * dx + inner
                    term = term + products[r, x + dx, 8 * k : 8 * k + 8, :] * rolled[k, x : x + 1, :]
                total = total + pltpu.roll(term, (-16 * dy - dz) % 128, 1)
            near_ref[:, r, x, :] = total


def shifted_rows(block, shift, valid):
    moved = pltpu.roll(block, (-shift) % 8, 0) if shift % 8 else block
    return jnp.where(valid, moved, 0.0)


def downward(
    where, lists, one, halo_one, two, halo_two, three, halo_three, table_one, table_two, table_three,
    phase_three, back_two, up_three, phase_two, far_high, far_low,
    partial_ref,
    ext_one, ext_two, ext_three,
):
    first, last = where[1] == 0, where[2] == 0
    first_two, last_two = where[1] < 2, where[2] < 2
    zero = jnp.zeros((8, 128), F32)
    z = iota((8, 128), 0)
    for shift in range(5):
        dz = shift - 2
        valid = (z + dz >= 0) & (z + dz < 8)
        for x in range(8):
            for y in (0, 1, 6, 7):
                ext_one[shift, x, y] = zero
            for y in range(4):
                row = 8 * y + 32 * (x % 2)
                if x < 2:
                    block = jnp.where(first, 0.0, halo_one[0, row : row + 8, :])
                elif x > 5:
                    block = jnp.where(last, 0.0, halo_one[1, row : row + 8, :])
                else:
                    block = one[32 * (x - 2) + 8 * y : 32 * (x - 2) + 8 * y + 8, :]
                ext_one[shift, x, y + 2] = shifted_rows(block, dz, valid)
    zero = jnp.zeros((8, 512), F32)
    y, z = iota((8, 512), 0) // 4, iota((8, 512), 0) % 4
    for shift in range(25):
        dy, dz = shift // 5 - 2, shift % 5 - 2
        valid = (y + dy >= 0) & (y + dy < 2) & (z + dz >= 0) & (z + dz < 4)
        for x in range(6):
            if abs(dy) == 2:
                ext_two[shift, x] = zero
                continue
            row = 8 * (x % 2)
            if x < 2:
                block = jnp.where(first, 0.0, halo_two[0, row : row + 8, :])
            elif x > 3:
                block = jnp.where(last, 0.0, halo_two[1, row : row + 8, :])
            else:
                block = two[row : row + 8, :]
            ext_two[shift, x] = shifted_rows(block, 4 * dy + dz, valid)
    z = iota((8, 512), 0) % 2
    for x in range(5):
        if x == 2:
            block = three[...]
        else:
            missing = (first_two, first, None, last, last_two)[x]
            block = jnp.where(missing, 0.0, halo_three[(0, 1, None, 2, 3)[x]])
        for shift in range(3):
            dz = shift - 1
            ext_three[shift, x] = shifted_rows(block, dz, (z + dz >= 0) & (z + dz < 2))
        ext_three[3, x] = zero

    real = jnp.zeros((4, 4, 8, 128), F32)
    imag = jnp.zeros((4, 4, 8, 128), F32)
    for k in range(32):
        dx, dy, dz = lists[3 * k], lists[3 * k + 1], lists[3 * k + 2]
        window = ext_one[dz + 2, pl.ds(dx + 2, 4), pl.ds(dy + 2, 4)]
        real = real + window * table_one[2 * k : 2 * k + 1, :]
        imag = imag + window * table_one[2 * k + 1 : 2 * k + 2, :]
    imag = imag.reshape(128, 128)
    turned_imag = pltpu.roll(imag, 64, 1)
    field = real.reshape(128, 128) + jnp.where(iota((128, 128), 1) < 64, -turned_imag, turned_imag)
    field_one = field.T

    reals = [jnp.zeros((2, 8, 128), F32) for _ in range(4)]
    for k in range(32):
        dx, dy, dz = lists[96 + 3 * k], lists[97 + 3 * k], lists[98 + 3 * k]
        window = ext_two[5 * dy + dz + 12, pl.ds(dx + 2, 2)]
        x = table_two[2 * k : 2 * k + 1, :]
        y = table_two[2 * k + 1 : 2 * k + 2, :]
        parts = [window[:, :, 128 * i : 128 * i + 128] for i in range(4)]
        for r in range(2):
            reals[r] = reals[r] + (x * parts[r] - y * parts[2 + r])
            reals[2 + r] = reals[2 + r] + (x * parts[2 + r] + y * parts[r])
    side = jnp.zeros((64, 32), F32)
    field_two = jnp.concatenate([side, jnp.concatenate(reals, axis=0).reshape(64, 128), side], axis=1)

    real = jnp.zeros((8, 512), F32)
    imag = jnp.zeros((8, 512), F32)
    for k in range(32):
        dx, dy, dz = lists[192 + 3 * k], lists[193 + 3 * k], lists[194 + 3 * k]
        inside = (dy == 0) & (dz >= -1) & (dz <= 1)
        window = ext_three[jnp.where(inside, dz + 1, 3), dx + 2]
        real = real + window * table_three[2 * k : 2 * k + 1, :]
        imag = imag + window * table_three[2 * k + 1 : 2 * k + 2, :]
    imag = pltpu.roll(imag, 4, 0)
    incoming = real + jnp.where(iota((8, 512), 0) < 4, -imag, imag)

    row = iota((64, 8), 0)
    apart = onehot(row // 16 * 2 + row // 2 % 2 == iota((64, 8), 1))
    spread = dot_right(apart, incoming)
    cosine, sine = phase_three[0:16], phase_three[16:32]
    parts = []
    for c in range(2):
        for r in range(2):
            x, y = spread[16 * r : 16 * r + 16], spread[32 + 16 * r : 48 + 16 * r]
            parts.append(x * cosine + y * sine if c == 0 else y * cosine - x * sine)
    level_two = field_two + dot3(jnp.concatenate(parts, axis=0), up_three[...], ((1,), (1,)))
    parent = onehot(parent_of_box(iota((16, 128), 1)) == iota((16, 128), 0))
    columns = level_two.T
    spread = [dot_left(columns[:, 16 * i : 16 * i + 16], parent) for i in range(4)]
    cosine, sine = phase_two[:, :128], phase_two[:, 128:]
    real = jnp.concatenate([spread[r] * cosine + spread[2 + r] * sine for r in range(2)], axis=1)
    imag = jnp.concatenate([spread[2 + r] * cosine - spread[r] * sine for r in range(2)], axis=1)
    pad = jnp.zeros((32, 256), F32)
    level_one = []
    for c, value in enumerate((real, imag)):
        field = jnp.concatenate([field_one[64 * c + 32 * r : 64 * c + 32 * r + 32] for r in range(2)], axis=1)
        level_one.append(dot3(back_two[...], value) + jnp.concatenate([pad, field, pad], axis=0))
    high, low = split(jnp.concatenate(level_one, axis=0))
    for o in range(8):
        rows = slice(128 * o, 128 * o + 128)
        total = dot(far_high[rows], high) + (dot(far_high[rows], low) + dot(far_low[rows], high))
        for owner in range(16):
            partial_ref[owner % 2, owner // 4, owner // 2 % 2, 8 * o : 8 * o + 8, :] = total[
                8 * owner : 8 * owner + 8
            ]


def finish(far, near, unshuffle, out_ref):
    rows = []
    for r in range(2):
        for ox in range(2):
            pieces = [
                far[8 * (4 * ox + o) : 8 * (4 * ox + o) + 8, 128 * r : 128 * r + 128] for o in range(4)
            ]
            rows.append(jnp.concatenate(pieces, axis=1))
    leaf = dot_left(jnp.concatenate(rows, axis=0), unshuffle[...])
    for r in range(2):
        for ox in range(2):
            for x in range(4):
                row = 8 * (2 * r + ox)
                out_ref[:, r, 2 * x + ox, :] = (
                    near[:, r, 2 * x + ox, :] + leaf[row : row + 8, 128 * x : 128 * x + 128]
                )


def barrier(peers, maybe=()):
    sem = pltpu.get_barrier_semaphore()
    count = len(peers)
    for peer in peers:
        pl.semaphore_signal(sem, inc=1, device_id=peer, device_id_type=MESH)
    for condition, peer in maybe:
        @pl.when(condition)
        def _(peer=peer):
            pl.semaphore_signal(sem, inc=1, device_id=peer, device_id_type=MESH)

        count = count + jnp.where(condition, 1, 0)
    pl.semaphore_wait(sem, count)


def remote(source, target, send, receive, peer):
    return pltpu.make_async_remote_copy(
        src_ref=source, dst_ref=target, send_sem=send, recv_sem=receive, device_id=peer, device_id_type=MESH
    )


def gather_kernel(
    dirs, boxes, tables, to_next, to_previous, source,
    gathered, rims, halo,
    send, receive, rim_send, rim_receive, halo_send, halo_receive, local,
):
    me, box = lax.axis_index("dir"), lax.axis_index("box")
    peers = [{"dir": lax.rem(me + e, dirs)} for e in range(1, dirs)]
    has_left, has_right = box > 0, box < boxes - 1
    left, right = {"box": lax.rem(box + boxes - 1, boxes)}, {"box": lax.rem(box + 1, boxes)}
    own = pltpu.make_async_copy(tables.at[me], gathered.at[0], local)
    own.start()
    barrier(peers, ((has_left, left), (has_right, right)))
    to_right = remote(
        source.at[:, 1, :, pl.ds(384, 128)], halo.at[0], halo_send.at[0], halo_receive.at[0], right
    )
    to_left = remote(source.at[:, 0, :, pl.ds(0, 128)], halo.at[1], halo_send.at[1], halo_receive.at[1], left)
    copies = [
        remote(to_next, rims.at[0], rim_send.at[0], rim_receive.at[0], peers[0]),
        remote(to_previous, rims.at[1], rim_send.at[1], rim_receive.at[1], peers[-1]),
    ]
    for e in range(1, dirs):
        copies.append(
            remote(
                tables.at[lax.rem(me + e, dirs)], gathered.at[dirs - e], send.at[e], receive.at[dirs - e],
                peers[e - 1],
            )
        )
    for copy in copies:
        copy.start()
    pl.when(has_right)(to_right.start)
    pl.when(has_left)(to_left.start)
    for copy in copies:
        copy.wait_send()
    for copy in copies:
        copy.wait_recv()
    pl.when(has_right)(to_right.wait_send)
    pl.when(has_left)(to_left.wait_send)
    pl.when(has_left)(to_right.wait_recv)
    pl.when(has_right)(to_left.wait_recv)
    own.wait()


def halo_kernel(boxes, one, two, three, halo_one, halo_two, halo_three, send, receive):
    box = lax.axis_index("box")
    has = {-1: box > 0, 1: box < boxes - 1, -2: box > 1, 2: box < boxes - 2}
    peer = {e: {"box": lax.rem(box + boxes + e, boxes)} for e in has}
    barrier([], [(has[e], peer[e]) for e in has])
    copies = [
        (1, one.at[pl.ds(64, 64)], halo_one.at[0]),
        (-1, one.at[pl.ds(0, 64)], halo_one.at[1]),
        (1, two, halo_two.at[0]),
        (-1, two, halo_two.at[1]),
        (2, three, halo_three.at[0]),
        (1, three, halo_three.at[1]),
        (-1, three, halo_three.at[2]),
        (-2, three, halo_three.at[3]),
    ]
    made = [
        (e, remote(source, target, send.at[i], receive.at[i], peer[e]))
        for i, (e, source, target) in enumerate(copies)
    ]
    for e, copy in made:
        pl.when(has[e])(copy.start)
    for e, copy in made:
        pl.when(has[e])(copy.wait_send)
        pl.when(has[-e])(copy.wait_recv)


def sum_kernel(partial, total, got_core, held, got_x, held_x, got_z, send, receive):
    me = lax.axis_index("dir")
    x, z, core = me // 4, me // 2 % 2, me % 2
    sibling = {"dir": me + 1 - 2 * core}
    across = {"dir": me + 2 - 4 * z}
    others = [{"dir": lax.rem(me + 4 * e, 16)} for e in range(1, 4)]
    barrier([sibling, across] + others)
    copy = remote(partial.at[1 - core], got_core, send.at[0], receive.at[0], sibling)
    copy.start()
    copy.wait()
    held[...] = partial[core] + got_core[...]
    copies = [
        remote(held.at[lax.rem(x + e, 4)], got_x.at[3 - e], send.at[e], receive.at[4 - e], others[e - 1])
        for e in range(1, 4)
    ]
    for copy in copies:
        copy.start()
    for copy in copies:
        copy.wait_send()
    for copy in copies:
        copy.wait_recv()
    held_x[...] = held[x] + (got_x[0] + got_x[1] + got_x[2])
    copy = remote(held_x.at[1 - z], got_z, send.at[4], receive.at[4], across)
    copy.start()
    copy.wait()
    total[...] = held_x[z] + got_z[...]


ANY = pl.BlockSpec(memory_space=pl.ANY)
VMEM = pl.BlockSpec(memory_space=pltpu.VMEM)
SMEM = pl.BlockSpec(memory_space=pltpu.SMEM)
DMA = pltpu.SemaphoreType.DMA


def shape(*dims, dtype=F32):
    return jax.ShapeDtypeStruct(dims, dtype)


def communicate(kernel, collective_id, in_specs, out_specs, out_shape, scratch, *args):
    return pl.pallas_call(
        kernel,
        out_shape=out_shape,
        in_specs=in_specs,
        out_specs=out_specs,
        scratch_shapes=scratch,
        compiler_params=pltpu.CompilerParams(
            collective_id=collective_id, has_side_effects=True, vmem_limit_bytes=VMEM_LIMIT
        ),
    )(*args)


def compute(kernel, scalars, out_shape, scratch, *args):
    specs = [SMEM] * scalars + [VMEM] * (len(args) - scalars)
    return pl.pallas_call(
        kernel,
        out_shape=out_shape,
        in_specs=specs,
        out_specs=jax.tree.map(lambda _: VMEM, out_shape),
        scratch_shapes=scratch,
        compiler_params=pltpu.CompilerParams(vmem_limit_bytes=VMEM_LIMIT),
    )(*args)


def gather_tables(tables, to_next, to_previous, source):
    dirs, boxes = lax.axis_size("dir"), lax.axis_size("box")
    return communicate(
        functools.partial(gather_kernel, dirs, boxes), 1, [ANY] * 4, [ANY] * 3,
        [shape(16, 16, 128, dtype=BF16), shape(2, 32, 128), shape(2, 2, 128, 128, dtype=BF16)],
        [DMA((16,)), DMA((16,)), DMA((2,)), DMA((2,)), DMA((2,)), DMA((2,)), DMA],
        tables, to_next, to_previous, source,
    )


def exchange_halos(one, two, three):
    boxes = lax.axis_size("box")
    return communicate(
        functools.partial(halo_kernel, boxes), 2, [ANY] * 3, [ANY] * 3,
        [shape(2, 64, 128), shape(2, 16, 512), shape(4, 8, 512)],
        [DMA((8,)), DMA((8,))],
        one, two, three,
    )


def sum_over_dirs(partial):
    return communicate(
        sum_kernel, 3, [VMEM], VMEM, shape(64, 256),
        [
            pltpu.VMEM((4, 2, 64, 256), F32), pltpu.VMEM((4, 2, 64, 256), F32),
            pltpu.VMEM((3, 2, 64, 256), F32), pltpu.VMEM((2, 64, 256), F32), pltpu.VMEM((64, 256), F32),
            DMA((5,)), DMA((5,)),
        ],
        partial,
    )


def shuffle_table():
    index = np.arange(512)
    x, y, z = index // 128, index // 16 % 8, index % 16
    target = 256 * (y % 2) + 128 * (z % 2) + 32 * x + 8 * (y // 2) + z // 2
    return (target[:, None] == index[None, :]).astype(np.float32)


def turn_table(angles):
    rows = jnp.transpose(angles, (2, 1, 0)).reshape(-1, 8)
    return jnp.concatenate([jnp.cos(rows), jnp.sin(rows)], axis=1)


def to_lanes(table, copies):
    flat = jnp.transpose(table, (0, 1, 3, 2)).reshape(64, -1)
    return jnp.tile(flat, (1, copies))


def shards(
    source, near_blocks, near_mask, radiate, receive, theta_one, theta_two, theta_three, phi_taps,
    shift_one, shift_two, shift_three, trans_one, trans_two, trans_three, far_lists,
):
    dirs, boxes = lax.axis_size("dir"), lax.axis_size("box")
    me, box = lax.axis_index("dir"), lax.axis_index("box")
    where = jnp.stack([me, box, boxes - 1 - box]).astype(jnp.int32)
    layers = source.reshape(64, 2, 2, 4, 2, 128)
    layers = jnp.transpose(layers, (2, 4, 0, 1, 3, 5)).reshape(2, 2, 128, 512)
    taps = phi_taps.reshape(18)
    lists = far_lists.reshape(288)

    windows = jnp.transpose(receive, (2, 1, 3, 0))
    windows = jnp.stack([jnp.roll(windows, 2 - a, axis=0) for a in range(5)], axis=2).reshape(16, 8, 40)
    windows = jnp.pad(windows, ((0, 0), (0, 0), (0, 88)))
    outgoing = jnp.transpose(radiate[:, :, 0], (1, 2, 0)).reshape(1, 8, 128)
    tables = jnp.concatenate([windows, jnp.broadcast_to(outgoing, (16, 8, 128))], axis=1)
    turn_one, turn_two = turn_table(shift_one), turn_table(shift_two)
    own_one = jnp.pad(turn_one, ((0, 0), (0, 112)))
    own_two = jnp.pad(turn_two, ((0, 0), (0, 112)))
    to_next = jnp.pad(jnp.concatenate([turn_one, turn_two[96:]], axis=1), ((0, 0), (0, 96)))
    to_previous = jnp.pad(jnp.concatenate([turn_one, turn_two[:32]], axis=1), ((0, 0), (0, 96)))
    gathered, rims, halo = gather_tables(tables, to_next, to_previous, layers)

    angles = jnp.transpose(shift_three, (0, 2, 1)).reshape(2, 2, 1, 2, 512)
    angles = jnp.broadcast_to(angles, (2, 2, 2, 2, 512)).reshape(16, 512)
    phase_three = jnp.concatenate([jnp.cos(angles), jnp.sin(angles)], axis=0)
    shuffle = shuffle_table()
    one, two, three, back_two, up_three, phase_two, far_high, far_low = compute(
        upward, 2,
        [
            shape(128, 128), shape(16, 512), shape(8, 512), shape(96, 192), shape(192, 512),
            shape(192, 256), shape(1024, 192, dtype=BF16), shape(1024, 192, dtype=BF16),
        ],
        [pltpu.VMEM((1024, 256), BF16), pltpu.VMEM((192, 1024), BF16), pltpu.VMEM((192, 1024), BF16)],
        where, taps, layers, jnp.asarray(shuffle, BF16), gathered, rims, own_one, own_two, phase_three,
        theta_one, theta_two, theta_two.T, theta_three.T,
    )
    halo_one, halo_two, halo_three = exchange_halos(one, two, three)

    b_real, b_imag = near_blocks[:, 0], near_blocks[:, 1]
    rows = jnp.stack([jnp.stack([b_real, -b_imag], axis=-1), jnp.stack([b_imag, b_real], axis=-1)], axis=2)
    near = compute(
        near_part, 1, shape(8, 2, 8, 128),
        [pltpu.VMEM((2, 10, 216, 128), F32), pltpu.VMEM((27, 8, 128), F32)],
        where, layers, halo, rows.reshape(216, 128), near_mask,
    )
    partial = compute(
        downward, 2, shape(2, 4, 2, 64, 256),
        [
            pltpu.VMEM((5, 8, 8, 8, 128), F32), pltpu.VMEM((25, 6, 8, 512), F32),
            pltpu.VMEM((4, 5, 8, 512), F32),
        ],
        where, lists, one, halo_one, two, halo_two, three, halo_three,
        to_lanes(trans_one, 4), to_lanes(trans_two, 1), to_lanes(trans_three, 1),
        phase_three, back_two, up_three, phase_two, far_high, far_low,
    )
    far = sum_over_dirs(partial)
    out = compute(finish, 0, shape(8, 2, 8, 128), [], far, near, jnp.asarray(shuffle.T, BF16))
    return out.reshape(4, 2, 2, 8, 128)


def solution(mesh):
    placed = (
        P(None, None, None, "box", None),
        P(None, None, "dir", None),
        P(None, "box", None),
        P(None, None, "dir", None),
        P(None, None, None, "dir"),
        P(),
        P(),
        P(),
        P(),
        P(None, None, "dir"),
        P(None, None, "dir"),
        P(None, None, "dir"),
        P(None, None, None, "dir"),
        P(None, None, None, "dir"),
        P(None, None, None, "dir"),
        P(),
    )
    return jax.shard_map(
        shards,
        mesh=mesh,
        in_specs=placed,
        out_specs=P("dir", None, None, "box", None),
        check_vma=False,
    )
```

time: 558 us -> 112 us (0.20)
  the two profiles are of different devices: /device:TPU:1 before, /device:TPU:103 now
where the time goes in v1:
time: 112 us; the launch traced here: 111 us
  Pallas kernels  75.8 us (68%)
  local copies, waits for them, and re-layouts  31.2 us (28%)
  other arithmetic  3.94 us (4%)
    pallas_call x3, Pallas kernels, communicate(): pl.pallas_call(kernel, out_shape=out_shape, in_specs=in_specs, out_specs=...  61.9 us
    pallas_call x4, Pallas kernels, compute(): pl.pallas_call(kernel, out_shape=out_shape, in_specs=specs, out_specs=jax...  13.8 us
    reshape x1, local copies, waits for them, and re-layouts, shards(): rows.reshape(216, 128)  6.5 us
    unnamed x11, local copies, waits for them, and re-layouts  4.25 us
    slice x4, local copies, waits for them, and re-layouts, shards(): jnp.roll(windows, 2 - a, axis=0)  3.5 us
    another operation x6, local copies, waits for them, and re-layouts, to_lanes(): return jnp.tile(flat, (1, copies))  3.29 us
    another operation x1, local copies, waits for them, and re-layouts, shards(): jnp.stack([jnp.stack([b_real, -b_imag], axis=-1), jnp.stack([b_imag, b_re...  2.72 us

profile of v1, /device:TPU:103, one launch (start us, length us, event | category | flops | bytes accessed | tf_op | source)
XLA Modules:
  0.0 111.1 jit_solution(16315273504701850003)
XLA Ops:
  0.0 0.0 copy-start.2
  0.0 0.0 copy-start
  0.0 0.6 pad_add_fusion.where
  0.6 1.3 %reshape.51.taps = f32[18]{0:T(128)} reshape(f32[3,2,3]{2,1,0:T(2,128)} %param.26) | data formatting | bytes 144 | tf_op jit(solution)/shard_map/reshape | solution.py:565
  1.9 1.4 %copy.57.theta_one = f32[16,8]{1,0:T(8,128)} copy(f32[16,8]{0,1:T(8,128)} %param.23) | data formatting | bytes 1024 | tf_op args[5]
  3.3 1.4 %copy.58.theta_two = f32[32,16]{1,0:T(8,128)} copy(f32[32,16]{0,1:T(8,128)} %param.24) | data formatting | bytes 4096 | tf_op args[6]
  4.6 0.8 cosine_bitcast_fusion.2
  5.5 0.1 copy.52
  5.6 0.1 copy.53
  5.6 0.7 select_maximum_fusion.own_one
  6.3 0.8 fusion.6
  7.1 0.8 copy.50
  7.9 0.1 copy.51
  7.9 1.7 %tile_reshape.7.table_two = f32[64,128]{1,0:T(8,128)} reshape(f32[32,2,4,32]{3,2,1,0:T(4,128)} %bitcast.86) | data formatting | bytes 65536 | tf_op jit(solution)/shard_map/tile;reshape | solution.py:553
  9.6 0.8 cosine_bitcast_fusion.1
  10.4 0.1 cos.36
  10.5 0.1 sin.36
  10.6 0.9 fusion.8
  11.5 0.9 fusion.11
  12.4 0.9 fusion.10
  13.2 0.9 fusion.9
  14.1 0.8 copy.46
  14.9 0.7 reshape.50.lists
  15.6 0.8 slice_bitcast_fusion
  16.4 0.1 maximum_bitcast_fusion
  16.5 0.7 pad_maximum_fusion
  17.2 0.1 copy.54
  17.4 0.6 pad.23.own_two
  18.0 0.1 pad_maximum_fusion.3
  18.1 0.6 pad.21.to_previous
  18.7 0.6 pad.20.to_next
  19.3 0.1 fusion.2
  19.4 0.1 fusion.3
  19.5 0.7 constant_dynamic-update-slice_fusion
  20.2 0.1 fusion.4
  20.3 0.1 fusion.5
  20.4 0.1 copy.49
  20.5 0.6 fusion.1.tables
  21.2 0.9 copy.59
  22.0 0.1 tile.10
  22.1 0.1 copy.60
  22.2 0.7 copy.61.table_one
  22.9 0.9 sine_bitcast_fusion
  23.8 0.1 sin.39
  23.9 0.1 cos.39
  24.1 0.0 copy-done.2
  24.1 0.0 copy-start.1
  24.1 0.8 tile_reshape.8.table_three
  24.9 0.0 copy-done
  24.9 0.1 copy.66
  25.0 1.0 reshape.53.source
  26.0 22.7 %shard_map.172 = (bf16[16,16,128]{2,1,0:T(8,128)(2,1)}, f32[2,32,128]{2,1,0:T(8,128)}, bf16[2,2,128,128]{3,2,1,0:T(8,128)(2,1)}) custom-call(bf16[16,16,128]{2,1,0:T(8,128)(2,1)} %fusion.1.tables, f32[32,128]{1,0:T(8,128)} %pad.20.to_next, f32[32,128]{1,0:T(8,128)} %pad.21.to_previous, bf16[2,2,128,512]{3,2,1,0:T(8,128)(2,1)} %reshape.53.source), custom_call_target="tpu_custom_call" | custom-call | tf_op jit(solution)/shard_map/pallas_call | solution.py:483
  48.8 0.0 copy-done.1
  48.8 4.2 %shard_map.173 = (f32[128,128]{1,0:T(8,128)}, f32[16,512]{1,0:T(8,128)}, f32[8,512]{1,0:T(8,128)}, f32[96,192]{1,0:T(8,128)}, f32[192,512]{1,0:T(8,128)}, /*inde...) custom-call(s32[3]{0:T(128)} %pad_add_fusion.where, f32[18]{0:T(128)} %reshape.51.taps, ...), custom_call_target="tpu_custom_call" | custom-call | tf_op jit(solution)/shard_map/pallas_call | solution.py:497
  53.0 8.6 %shard_map.174 = (f32[2,64,128]{2,1,0:T(8,128)}, f32[2,16,512]{2,1,0:T(8,128)}, f32[4,8,512]{2,1,0:T(8,128)}) custom-call(f32[128,128]{1,0:T(8,128)} %get-tuple-element.21.one, f32[16,512]{1,0:T(8,128)} %get-tuple-element.22.two, f32[8,512]{1,0:T(8,128)} %get-tuple-element.23.three), custom_call_target="tpu_custom_call" | custom-call | tf_op jit(solution)/shard_map/pallas_call | solution.py:483
  61.6 5.2 %shard_map.175.partial = f32[2,4,2,64,256]{4,3,2,1,0:T(8,128)} custom-call(s32[3]{0:T(128)} %pad_add_fusion.where, s32[288]{0:T(512)} %reshape.50.lists, f32[128,128]{1,0:T(8,128)} %get-tuple-element.21.one, f32[2,64,128]{2,1,0:T(8,128)} %get-tuple-element.24.halo_one, f32[16,512]{1,0:T(8,128)} %get-tuple-element.22.two, ...), custom_call_target="tpu_custom_call" | custom-call | tf_op jit(solution)/shard_map/pallas_call | solution.py:497
  66.8 30.6 %shard_map.176.far = f32[64,256]{1,0:T(8,128)} custom-call(f32[2,4,2,64,256]{4,3,2,1,0:T(8,128)} %shard_map.175.partial), custom_call_target="tpu_custom_call" | custom-call | tf_op jit(solution)/shard_map/pallas_call | solution.py:483
  97.4 2.7 %copy.63 = bf16[27,4,2,64,2]{4,3,2,1,0:T(8,128)(2,1)S(1)} copy(bf16[27,4,2,64,2]{3,1,0,4,2:T(4,128)(2,1)} %pad_maximum_fusion) | data formatting | bytes 110592 | tf_op jit(solution)/shard_map/stack | solution.py:597
  100.2 6.5 %reshape.55.blocks = bf16[216,128]{1,0:T(8,128)(2,1)} reshape(bf16[27,4,2,64,2]{4,3,2,1,0:T(8,128)(2,1)S(1)} %copy.63) | data formatting | bytes 110592 | tf_op jit(solution)/shard_map/reshape | solution.py:601
  106.7 2.4 %shard_map.177.near = f32[8,2,8,128]{3,2,1,0:T(8,128)} custom-call(s32[3]{0:T(128)} %pad_add_fusion.where, bf16[2,2,128,512]{3,2,1,0:T(8,128)(2,1)} %reshape.53.source, bf16[2,2,128,128]{3,2,1,0:T(8,128)(2,1)} %get-tuple-element.32.halo, bf16[216,128]{1,0:T(8,128)(2,1)} %reshape.55.blocks, s32[27,8,128]{2,1,0:T(8,128)} %mask.1), custom_call_target="tpu_custom_call" | custom-call | tf_op jit(solution)/shard_map/pallas_call | solution.py:497
  109.0 2.1 %shard_map.178 = f32[8,2,8,128]{3,2,1,0:T(8,128)} custom-call(f32[64,256]{1,0:T(8,128)} %shard_map.176.far, f32[8,2,8,128]{3,2,1,0:T(8,128)} %shard_map.177.near, bf16[512,512]{1,0:T(8,128)(2,1)} %constant.21.clone.unshuffle), custom_call_target="tpu_custom_call" | custom-call | tf_op jit(solution)/shard_map/pallas_call | solution.py:497
  (11 shorter events, 0.1 us)
Async XLA Ops:
  0.0 24.1 %copy-start.2 = (f32[32,2,64,8]{2,3,1,0:T(8,128)S(1)}, f32[32,2,64,8]{2,3,1,0:T(8,128)}, u32[]{:S(2)}) copy-start(f32[32,2,64,8]{2,3,1,0:T(8,128)} %param.32) | copy-start | bytes 393220
  0.0 24.9 %copy-start = (bf16[64,2,2,8,128]{4,3,2,1,0:T(8,128)(2,1)S(1)}, bf16[64,2,2,8,128]{4,3,2,1,0:T(8,128)(2,1)}, u32[]{:S(2)}) copy-start(bf16[64,2,2,8,128]{4,3,2,1,0:T(8,128)(2,1)} %param.18) | copy-start | bytes 1572868
  24.1 24.7 %copy-start.1 = (f32[32,512]{1,0:T(8,128)}, f32[32,512]{1,0:T(8,128)S(1)}, u32[]{:S(2)}) copy-start(f32[32,512]{1,0:T(8,128)S(1)} %constant_dynamic-update-slice_fusion.1.phase_three) | copy-start | bytes 196612

commit v2 on v1

v2 whole, which is shorter than its diff:
```python
import functools

import jax
import jax.numpy as jnp
import numpy as np
from jax import lax
from jax.experimental import pallas as pl
from jax.experimental.pallas import tpu as pltpu
from jax.sharding import PartitionSpec as P

MESH = pl.DeviceIdType.MESH
F32 = jnp.float32
BF16 = jnp.bfloat16
VMEM_LIMIT = 56 * 1024 * 1024


def iota(shape, dim):
    return lax.broadcasted_iota(jnp.int32, shape, dim)


def split(a):
    high = a.astype(BF16)
    return high, (a - high.astype(F32)).astype(BF16)


def dot(a, b, dims=((1,), (0,))):
    return lax.dot_general(a, b, (dims, ((), ())), preferred_element_type=F32)


def dot3(a, b, dims=((1,), (0,))):
    a_high, a_low = split(a)
    b_high, b_low = split(b)
    return dot(a_high, b_high, dims) + (dot(a_high, b_low, dims) + dot(a_low, b_high, dims))


def dot_left(a, b, dims=((1,), (0,))):
    a_high, a_low = split(a)
    return dot(a_high, b, dims) + dot(a_low, b, dims)


def dot_right(a, b, dims=((1,), (0,))):
    b_high, b_low = split(b)
    return dot(a, b_high, dims) + dot(a, b_low, dims)


def onehot(condition):
    return jnp.where(condition, 1.0, 0.0).astype(BF16)


def interpolation(taps, level, theta, fine, coarse, wide, first, transposed):
    (fine_p, fine_t), (coarse_p, coarse_t) = fine, coarse
    if transposed:
        spread = onehot(iota((fine_t, fine_p * fine_t), 1) % fine_t == iota((fine_t, fine_p * fine_t), 0))
        tiled = jnp.concatenate([dot_left(theta, spread)] * coarse_p, axis=0)
        fine_dim, coarse_dim = 1, 0
    else:
        spread = onehot(
            iota((coarse_t, coarse_p * coarse_t), 1) % coarse_t == iota((coarse_t, coarse_p * coarse_t), 0)
        )
        tiled = jnp.concatenate([dot_left(theta, spread)] * fine_p, axis=0)
        fine_dim, coarse_dim = 0, 1
    p = iota(tiled.shape, fine_dim) // fine_t
    tap = iota(tiled.shape, coarse_dim) // coarse_t - first(p)
    even = wide(p) % 2 == 0
    weight = jnp.zeros(tiled.shape, F32)
    for j in range(3):
        value = jnp.where(even, taps[level, 0:1, j : j + 1], taps[level, 1:2, j : j + 1])
        weight = jnp.where(tap == j, value, weight)
    return weight * tiled


def turned(x):
    even = iota(x.shape, 1) % 2 == 0
    count = x.shape[1]
    return jnp.where(even, -pltpu.roll(x, count - 1, 1), pltpu.roll(x, 1, 1))


def child_of_box(index):
    return 4 * (index // 32 % 2) + 2 * (index // 8 % 2) + index % 2


def parent_of_box(index):
    return index // 64 * 8 + index // 16 % 2 * 4 + index // 2 % 4


def shifted_rows(block, shift, valid):
    moved = pltpu.roll(block, (-shift) % 8, 0) if shift % 8 else block
    return jnp.where(valid, moved, 0.0)


def cosines(angles):
    return jnp.concatenate([jnp.cos(angles), jnp.sin(angles)], axis=0)


def remote(source, target, send, receive, peer):
    return pltpu.make_async_remote_copy(
        src_ref=source, dst_ref=target, send_sem=send, recv_sem=receive, device_id=peer, device_id_type=MESH
    )


def whole(
    dirs, boxes,
    source, near_blocks, mask, radiate, receive, theta_one, theta_two, theta_two_t, theta_three_t, taps,
    shift_one, shift_two, shift_three, trans_one, trans_two, trans_three, lists, shuffle,
    out_ref,
    message, gathered, rim_out, rims, leaf_halo, halo_one, halo_two, halo_three, one, two, three,
    leaf, shape_high, shape_low, far_high, far_low, products, rolled, near,
    table_one, table_two, table_three, ext_one, ext_two, ext_three,
    partial, got_core, held, got_x, held_x, got_z,
    send, receive_sem, rim_send, rim_receive, leaf_send, leaf_receive, halo_send, halo_receive,
    sum_send, sum_receive,
):
    me, box = lax.axis_index("dir"), lax.axis_index("box")
    has = {-1: box > 0, 1: box < boxes - 1, -2: box > 1, 2: box < boxes - 2}
    beside = {e: {"box": lax.rem(box + boxes + e, boxes)} for e in has}
    peers = {e: {"dir": lax.rem(me + e, dirs)} for e in range(1, dirs)}

    barrier = pltpu.get_barrier_semaphore()
    count = dirs - 1
    for e in range(1, dirs):
        pl.semaphore_signal(barrier, inc=1, device_id=peers[e], device_id_type=MESH)
    for e in has:
        @pl.when(has[e])
        def _(e=e):
            pl.semaphore_signal(barrier, inc=1, device_id=beside[e], device_id_type=MESH)

        count = count + jnp.where(has[e], 1, 0)

    taken = [receive[c, :, u, :].astype(F32) for c in range(2) for u in range(4)]
    lane = iota((64, 128), 1)
    sent = [dot(radiate[c], onehot(lane == 2 * iota((64, 128), 0) + c)) for c in range(2)]
    tile = jnp.concatenate([jnp.concatenate(taken, axis=1), sent[0] + sent[1]], axis=0).astype(BF16)
    message[...] = tile
    gathered[0] = tile
    angles_one = jnp.concatenate([shift_one[:, a, :] for a in range(2)], axis=1)
    angles_two = jnp.concatenate([shift_two[:, a, :] for a in range(4)], axis=1)
    pad = jnp.zeros((8, 64), F32)
    rim_out[0] = jnp.concatenate([angles_one, angles_two[:, 96:], pad], axis=1)
    rim_out[1] = jnp.concatenate([angles_one, angles_two[:, :32], pad], axis=1)

    up_one = interpolation(
        taps, 0, theta_one[...], (6, 16), (5, 8), lambda p: p, lambda p: p // 2, False
    )
    up_two = interpolation(
        taps, 1, theta_two[...], (6, 32), (6, 16), lambda p: p + 1, lambda p: (p + 1) // 2, False
    )
    back_two = interpolation(
        taps, 1, theta_two_t[...], (6, 32), (6, 16), lambda p: p + 1, lambda p: (p + 1) // 2, True
    )
    up_three = interpolation(
        taps, 2, theta_three_t[...], (8, 64), (6, 32), lambda p: p, lambda p: p // 2, True
    )
    for r in range(2):
        for ox in range(2):
            mixed = dot(source[r, ox], shuffle[...]).astype(BF16)
            for o in range(4):
                row = 128 * (4 * ox + o)
                leaf[row : row + 128, 128 * r : 128 * r + 128] = mixed[:, 128 * o : 128 * o + 128]
    for a in range(8):
        table_three[:, 64 * a : 64 * a + 64] = trans_three[:, a, :]
    for a in range(4):
        table_two[:, 32 * a : 32 * a + 32] = trans_two[:, a, :]
    for c in range(2):
        total = jnp.zeros((32, 128), F32)
        for a in range(2):
            place = onehot(iota((16, 128), 1) % 32 == 16 * a + iota((16, 128), 0))
            total = total + dot_left(trans_one[c, :, a, :], place, ((0,), (0,)))
        table_one[c] = total
    zero = jnp.zeros((8, 128), F32)
    for shift in range(5):
        for x in range(8):
            for y in (0, 1, 6, 7):
                ext_one[shift, x, y] = zero
    zero = jnp.zeros((8, 512), F32)
    for x in range(6):
        for shift in range(5):
            ext_two[shift, x] = zero
            ext_two[20 + shift, x] = zero
    for x in range(5):
        ext_three[3, x] = zero
    for side, e in enumerate((-1, 1)):
        @pl.when(jnp.logical_not(has[e]))
        def _(side=side):
            leaf_halo[side] = jnp.zeros((2, 128, 128), BF16)
            halo_one[side] = jnp.zeros((64, 128), F32)
            halo_two[side] = jnp.zeros((16, 512), F32)
    for slot, e in enumerate((-2, -1, 1, 2)):
        @pl.when(jnp.logical_not(has[e]))
        def _(slot=slot):
            halo_three[slot] = jnp.zeros((8, 512), F32)

    pl.semaphore_wait(barrier, count)
    table_copies = [
        remote(rim_out.at[0], rims.at[0], rim_send.at[0], rim_receive.at[0], peers[1]),
        remote(rim_out.at[1], rims.at[1], rim_send.at[1], rim_receive.at[1], peers[dirs - 1]),
    ]
    for e in range(1, dirs):
        table_copies.append(
            remote(message, gathered.at[dirs - e], send.at[e], receive_sem.at[dirs - e], peers[e])
        )
    for copy in table_copies:
        copy.start()
    leaf_copies = [
        (1, remote(
            source.at[:, 1, :, pl.ds(384, 128)], leaf_halo.at[0], leaf_send.at[0], leaf_receive.at[0], beside[1]
        )),
        (-1, remote(
            source.at[:, 0, :, pl.ds(0, 128)], leaf_halo.at[1], leaf_send.at[1], leaf_receive.at[1], beside[-1]
        )),
    ]
    for e, copy in leaf_copies:
        pl.when(has[e])(copy.start)

    lane = iota((64, 128), 1)
    double = dot(near_blocks[...], onehot(lane // 2 == iota((64, 128), 0))).astype(BF16)
    row, column = iota((216, 216), 0), iota((216, 216), 1)
    same = 8 * (row // 8) + 4 * (row % 2) + row % 8 // 2
    other = 8 * (row // 8) + 4 * (1 - row % 2) + row % 8 // 2
    kept = dot(onehot(column == same), double)
    crossed = dot(onehot(column == other), double)
    crossed = jnp.where(iota((216, 128), 0) % 2 == 0, -crossed, crossed)
    blocks = jnp.where(iota((216, 128), 1) % 2 == 0, kept, crossed).astype(BF16)
    lane = iota((8, 128), 1)
    for k in range(27):
        dy, dz = k // 3 % 3 - 1, k % 3 - 1
        y, z = lane // 16 + dy, lane % 16 + dz
        valid = (y >= 0) & (y < 8) & (z >= 0) & (z < 16)
        values = jnp.where(valid, mask[k].astype(F32), 0.0)
        rolled[k] = pltpu.roll(values, (16 * dy + dz) % 128, 1)
    for r in range(2):
        for ox in range(2):
            layers = dot(blocks, source[r, ox])
            for x in range(4):
                products[r, 1 + 2 * x + ox] = layers[:, 128 * x : 128 * x + 128]
    for e, copy in leaf_copies:
        pl.when(has[e])(copy.wait_send)
        pl.when(has[-e])(copy.wait_recv)
    for r in range(2):
        for side in range(2):
            products[r, 9 * side] = dot(blocks, leaf_halo[side, r])
    for r in range(2):
        for x in range(8):
            total = jnp.zeros((8, 128), F32)
            for inner in range(9):
                dy, dz = inner // 3 - 1, inner % 3 - 1
                term = jnp.zeros((8, 128), F32)
                for dx in range(3):
                    k = 9 * dx + inner
                    term = term + products[r, x + dx, 8 * k : 8 * k + 8, :] * rolled[k, x : x + 1, :]
                total = total + pltpu.roll(term, (-16 * dy - dz) % 128, 1)
            near[r, x] = total

    for copy in table_copies:
        copy.wait_send()
    for copy in table_copies:
        copy.wait_recv()
    pad = jnp.zeros((8, 32), F32)
    angles = jnp.concatenate([rims[0, :, 0:32], angles_one, rims[1, :, 0:32], pad], axis=1)
    turns = cosines(angles).T
    tables = gathered[...].astype(F32)
    sources = jnp.concatenate([tables[(a - 2) % 16, 8:16] for a in range(5)], axis=0)
    send_real = dot_left(up_one, sources.astype(BF16))
    send_turned = turned(send_real)
    even = iota((96, 128), 1) % 2 == 0
    for o in range(8):
        moved = turns[:96, o : o + 1] * send_real + turns[:96, 8 + o : 9 + o] * send_turned
        swapped = jnp.where(even, pltpu.roll(moved, 127, 1), pltpu.roll(moved, 1, 1))
        rows = jnp.concatenate([jnp.where(even, moved, -moved), swapped], axis=0)
        high, low = split(rows)
        shape_high[:, 128 * o : 128 * o + 128] = high
        shape_low[:, 128 * o : 128 * o + 128] = low
    level_one = dot(shape_high[...], leaf[...]) + dot(shape_low[...], leaf[...])
    own = jnp.concatenate(
        [level_one[96 * c + 32 : 96 * c + 64, 128 * r : 128 * r + 128] for c in range(2) for r in range(2)],
        axis=0,
    )
    one[...] = own.T
    halo_copies = [
        (e, remote(origin, target, halo_send.at[i], halo_receive.at[i], beside[e]))
        for i, (e, origin, target) in enumerate([
            (1, one.at[pl.ds(64, 64)], halo_one.at[0]),
            (-1, one.at[pl.ds(0, 64)], halo_one.at[1]),
            (1, two, halo_two.at[0]),
            (-1, two, halo_two.at[1]),
            (2, three, halo_three.at[0]),
            (1, three, halo_three.at[1]),
            (-1, three, halo_three.at[2]),
            (-2, three, halo_three.at[3]),
        ])
    ]
    for e, copy in halo_copies[:2]:
        pl.when(has[e])(copy.start)

    pad = jnp.zeros((8, 64), F32)
    angles = jnp.concatenate([rims[0, :, 32:64], angles_two, rims[1, :, 32:64], pad], axis=1)
    lane = iota((16, 256), 1)
    kind = child_of_box(lane % 128) + 8 * (lane // 128)
    phases = dot_left(cosines(angles).T[:192], onehot(iota((16, 256), 0) == kind))
    cosine_two, sine_two = phases[:, :128], phases[:, 128:]
    parent = onehot(parent_of_box(iota((16, 128), 1)) == iota((16, 128), 0))
    real = dot3(up_two, level_one[:96])
    imag = dot3(up_two, level_one[96:])
    parts = []
    for c in range(2):
        for r in range(2):
            x, y = real[:, 128 * r : 128 * r + 128], imag[:, 128 * r : 128 * r + 128]
            value = x * cosine_two - y * sine_two if c == 0 else y * cosine_two + x * sine_two
            parts.append(dot_right(parent, value, ((1,), (1,))))
    for index in range(4):
        two[:, 128 * index : 128 * index + 128] = parts[index][:, 32:160]
    for e, copy in halo_copies[2:4]:
        pl.when(has[e])(copy.start)
    level_two = jnp.concatenate(parts, axis=0)
    upper = dot3(level_two, up_three)
    turns_three = cosines(jnp.concatenate([shift_three[:, a, :] for a in range(8)], axis=1))
    row, column = iota((16, 8), 0), iota((16, 8), 1)
    expand = onehot(column == 4 * (row // 8) + 2 * (row // 4 % 2) + row % 2)
    cosine_three = dot_right(expand, turns_three[:8])
    sine_three = dot_right(expand, turns_three[8:])
    parts = []
    for c in range(2):
        for r in range(2):
            x, y = upper[16 * r : 16 * r + 16], upper[32 + 16 * r : 48 + 16 * r]
            parts.append(x * cosine_three - y * sine_three if c == 0 else y * cosine_three + x * sine_three)
    row = iota((8, 64), 1)
    together = onehot(row // 16 * 2 + row // 2 % 2 == iota((8, 64), 0))
    three[...] = dot_right(together, jnp.concatenate(parts, axis=0))
    for e, copy in halo_copies[4:]:
        pl.when(has[e])(copy.start)

    stacked = jnp.concatenate([tables[e, 0:8] for e in range(16)], axis=0)
    row, lane = iota((128, 640), 0), iota((128, 640), 1)
    azimuth = (me + 14 + lane // 128) % 16
    pick = onehot(row == 64 * (lane % 2) + 16 * (lane % 8 // 2) + azimuth)
    sender = (row // 8 + me) % 16
    placed = jnp.where(lane % 128 // 8 == sender, dot(stacked.astype(BF16), pick), 0.0)
    summed = placed[0:8]
    for e in range(1, 16):
        summed = summed + placed[8 * e : 8 * e + 8]
    targets = jnp.concatenate([summed[:, 128 * a : 128 * a + 128] for a in range(5)], axis=0)
    take_real = dot_left(up_one, targets.astype(BF16))
    take_turned = turned(take_real)
    for o in range(8):
        moved = turns[:96, o : o + 1] * take_real - turns[:96, 8 + o : 9 + o] * take_turned
        columns = jnp.concatenate([moved, turned(moved)], axis=0)
        high, low = split(columns.T)
        far_high[128 * o : 128 * o + 128, :] = high
        far_low[128 * o : 128 * o + 128, :] = low

    for e, copy in halo_copies[:2]:
        pl.when(has[-e])(copy.wait_recv)
    z = iota((8, 128), 0)
    for shift in range(5):
        dz = shift - 2
        valid = (z + dz >= 0) & (z + dz < 8)
        for x in range(8):
            for y in range(4):
                row = 8 * y + 32 * (x % 2)
                if x < 2 or x > 5:
                    block = halo_one[x // 4, row : row + 8, :]
                else:
                    block = one[32 * (x - 2) + 8 * y : 32 * (x - 2) + 8 * y + 8, :]
                ext_one[shift, x, y + 2] = shifted_rows(block, dz, valid)
    real = jnp.zeros((4, 4, 8, 128), F32)
    imag = jnp.zeros((4, 4, 8, 128), F32)
    for k in range(32):
        dx, dy, dz = lists[0, 0, k], lists[0, 1, k], lists[0, 2, k]
        window = ext_one[dz + 2, pl.ds(dx + 2, 4), pl.ds(dy + 2, 4)]
        real = real + window * table_one[0, k : k + 1, :]
        imag = imag + window * table_one[1, k : k + 1, :]
    imag = imag.reshape(128, 128)
    turned_imag = pltpu.roll(imag, 64, 1)
    field = real.reshape(128, 128) + jnp.where(iota((128, 128), 1) < 64, -turned_imag, turned_imag)
    field_one = field.T
    for e, copy in halo_copies[2:4]:
        pl.when(has[-e])(copy.wait_recv)
    y, z = iota((8, 512), 0) // 4, iota((8, 512), 0) % 4
    for shift in range(5, 20):
        dy, dz = shift // 5 - 2, shift % 5 - 2
        valid = (y + dy >= 0) & (y + dy < 2) & (z + dz >= 0) & (z + dz < 4)
        for x in range(6):
            row = 8 * (x % 2)
            if x < 2 or x > 3:
                block = halo_two[x // 3, row : row + 8, :]
            else:
                block = two[row : row + 8, :]
            ext_two[shift, x] = shifted_rows(block, 4 * dy + dz, valid)
    reals = [jnp.zeros((2, 8, 128), F32) for _ in range(4)]
    for k in range(32):
        dx, dy, dz = lists[1, 0, k], lists[1, 1, k], lists[1, 2, k]
        window = ext_two[5 * dy + dz + 12, pl.ds(dx + 2, 2)]
        x = table_two[2 * k : 2 * k + 1, :]
        y = table_two[2 * k + 1 : 2 * k + 2, :]
        parts = [window[:, :, 128 * i : 128 * i + 128] for i in range(4)]
        for r in range(2):
            reals[r] = reals[r] + (x * parts[r] - y * parts[2 + r])
            reals[2 + r] = reals[2 + r] + (x * parts[2 + r] + y * parts[r])
    side = jnp.zeros((64, 32), F32)
    field_two = jnp.concatenate([side, jnp.concatenate(reals, axis=0).reshape(64, 128), side], axis=1)
    for e, copy in halo_copies[4:]:
        pl.when(has[-e])(copy.wait_recv)
    z = iota((8, 512), 0) % 2
    for x in range(5):
        block = three[...] if x == 2 else halo_three[x - x // 3]
        for shift in range(3):
            dz = shift - 1
            ext_three[shift, x] = shifted_rows(block, dz, (z + dz >= 0) & (z + dz < 2))
    real = jnp.zeros((8, 512), F32)
    imag = jnp.zeros((8, 512), F32)
    for k in range(32):
        dx, dy, dz = lists[2, 0, k], lists[2, 1, k], lists[2, 2, k]
        inside = (dy == 0) & (dz >= -1) & (dz <= 1)
        window = ext_three[jnp.where(inside, dz + 1, 3), dx + 2]
        real = real + window * table_three[2 * k : 2 * k + 1, :]
        imag = imag + window * table_three[2 * k + 1 : 2 * k + 2, :]
    imag = pltpu.roll(imag, 4, 0)
    incoming = real + jnp.where(iota((8, 512), 0) < 4, -imag, imag)

    row = iota((64, 8), 0)
    apart = onehot(row // 16 * 2 + row // 2 % 2 == iota((64, 8), 1))
    spread = dot_right(apart, incoming)
    parts = []
    for c in range(2):
        for r in range(2):
            x, y = spread[16 * r : 16 * r + 16], spread[32 + 16 * r : 48 + 16 * r]
            parts.append(x * cosine_three + y * sine_three if c == 0 else y * cosine_three - x * sine_three)
    level_two = field_two + dot3(jnp.concatenate(parts, axis=0), up_three, ((1,), (1,)))
    columns = level_two.T
    spread = [dot_left(columns[:, 16 * i : 16 * i + 16], parent) for i in range(4)]
    real = jnp.concatenate([spread[r] * cosine_two + spread[2 + r] * sine_two for r in range(2)], axis=1)
    imag = jnp.concatenate([spread[2 + r] * cosine_two - spread[r] * sine_two for r in range(2)], axis=1)
    pad = jnp.zeros((32, 256), F32)
    level_one = []
    for c, value in enumerate((real, imag)):
        field = jnp.concatenate([field_one[64 * c + 32 * r : 64 * c + 32 * r + 32] for r in range(2)], axis=1)
        level_one.append(dot3(back_two, value) + jnp.concatenate([pad, field, pad], axis=0))
    high, low = split(jnp.concatenate(level_one, axis=0))

    x, z, core = me // 4, me // 2 % 2, me % 2
    sibling = {"dir": me + 1 - 2 * core}
    across = {"dir": me + 2 - 4 * z}
    others = [peers[4 * e] for e in range(1, 4)]
    to_core = [
        remote(partial.at[i, 1 - core], got_core.at[i], sum_send.at[i, 0], sum_receive.at[i, 0], sibling)
        for i in range(4)
    ]
    to_x = [
        [
            remote(
                held.at[i, lax.rem(x + e, 4)], got_x.at[i, 3 - e], sum_send.at[i, e], sum_receive.at[i, 4 - e],
                others[e - 1],
            )
            for e in range(1, 4)
        ]
        for i in range(4)
    ]
    to_z = [
        remote(held_x.at[i, 1 - z], got_z.at[i], sum_send.at[i, 4], sum_receive.at[i, 4], across)
        for i in range(4)
    ]

    def after_core(i):
        to_core[i].wait_recv()
        held[i] = partial[i, core] + got_core[i]
        for copy in to_x[i]:
            copy.start()

    for i in range(4):
        for o in (2 * i, 2 * i + 1):
            rows = slice(128 * o, 128 * o + 128)
            total = dot(far_high[rows], high) + (dot(far_high[rows], low) + dot(far_low[rows], high))
            for owner in range(16):
                partial[i, owner % 2, owner // 4, owner // 2 % 2, 8 * (o % 2) : 8 * (o % 2) + 8, :] = total[
                    8 * owner : 8 * owner + 8
                ]
        to_core[i].start()
        if i > 0:
            after_core(i - 1)
    after_core(3)
    for i in range(4):
        for copy in to_x[i]:
            copy.wait_recv()
        held_x[i] = held[i, x] + (got_x[i, 0] + got_x[i, 1] + got_x[i, 2])
        to_z[i].start()
    for e, copy in halo_copies:
        pl.when(has[e])(copy.wait_send)
    for i in range(4):
        to_core[i].wait_send()
        for copy in to_x[i]:
            copy.wait_send()
    far = []
    for i in range(4):
        to_z[i].wait_recv()
        far.append(held_x[i, z] + got_z[i])
    for i in range(4):
        to_z[i].wait_send()
    rows = []
    for r in range(2):
        for ox in range(2):
            pieces = [
                far[2 * ox + o // 2][8 * (o % 2) : 8 * (o % 2) + 8, 128 * r : 128 * r + 128] for o in range(4)
            ]
            rows.append(jnp.concatenate(pieces, axis=1))
    high, low = split(jnp.concatenate(rows, axis=0))
    both = dot(jnp.concatenate([high, low], axis=0), shuffle[...], ((1,), (1,)))
    far = both[:32] + both[32:]
    for r in range(2):
        for ox in range(2):
            for x in range(4):
                row = 8 * (2 * r + ox)
                out_ref[:, r, 2 * x + ox, :] = (
                    near[r, 2 * x + ox] + far[row : row + 8, 128 * x : 128 * x + 128]
                )


VMEM = pl.BlockSpec(memory_space=pltpu.VMEM)
SMEM = pl.BlockSpec(memory_space=pltpu.SMEM)
DMA = pltpu.SemaphoreType.DMA


def held_in(*dims, dtype=F32):
    return pltpu.VMEM(dims, dtype)


def shuffle_table():
    index = np.arange(512)
    x, y, z = index // 128, index // 16 % 8, index % 16
    target = 256 * (y % 2) + 128 * (z % 2) + 32 * x + 8 * (y // 2) + z // 2
    return (target[:, None] == index[None, :]).astype(np.float32)


def shards(
    source, near_blocks, near_mask, radiate, receive, theta_one, theta_two, theta_three, phi_taps,
    shift_one, shift_two, shift_three, trans_one, trans_two, trans_three, far_lists,
):
    dirs, boxes = lax.axis_size("dir"), lax.axis_size("box")
    layers = source.reshape(64, 2, 2, 4, 2, 128)
    layers = jnp.transpose(layers, (2, 4, 0, 1, 3, 5)).reshape(2, 2, 128, 512)
    args = (
        layers, near_blocks.reshape(216, 64), near_mask, radiate[:, :, 0], jnp.transpose(receive, (0, 1, 3, 2)),
        theta_one, theta_two, theta_two.T, theta_three.T, phi_taps,
        jnp.transpose(shift_one, (0, 2, 1)), jnp.transpose(shift_two, (0, 2, 1)),
        jnp.transpose(shift_three, (0, 2, 1)), jnp.transpose(trans_one, (1, 2, 3, 0)),
        jnp.transpose(trans_two, (0, 1, 3, 2)).reshape(64, 4, 32),
        jnp.transpose(trans_three, (0, 1, 3, 2)).reshape(64, 8, 64),
        jnp.transpose(far_lists, (0, 2, 1)), jnp.asarray(shuffle_table(), BF16),
    )
    specs = [VMEM] * len(args)
    specs[16] = SMEM
    out = pl.pallas_call(
        functools.partial(whole, dirs, boxes),
        out_shape=jax.ShapeDtypeStruct((8, 2, 8, 128), F32),
        in_specs=specs,
        out_specs=VMEM,
        scratch_shapes=[
            held_in(16, 128, dtype=BF16), held_in(16, 16, 128, dtype=BF16), held_in(2, 8, 128), held_in(2, 8, 128),
            held_in(2, 2, 128, 128, dtype=BF16), held_in(2, 64, 128), held_in(2, 16, 512), held_in(4, 8, 512),
            held_in(128, 128), held_in(16, 512), held_in(8, 512),
            held_in(1024, 256, dtype=BF16), held_in(192, 1024, dtype=BF16), held_in(192, 1024, dtype=BF16),
            held_in(1024, 192, dtype=BF16), held_in(1024, 192, dtype=BF16),
            held_in(2, 10, 216, 128), held_in(27, 8, 128), held_in(2, 8, 8, 128),
            held_in(2, 32, 128), held_in(64, 128), held_in(64, 512),
            held_in(5, 8, 8, 8, 128), held_in(25, 6, 8, 512), held_in(4, 5, 8, 512),
            held_in(4, 2, 4, 2, 16, 256), held_in(4, 4, 2, 16, 256), held_in(4, 4, 2, 16, 256),
            held_in(4, 3, 2, 16, 256), held_in(4, 2, 16, 256), held_in(4, 16, 256),
            DMA((16,)), DMA((16,)), DMA((2,)), DMA((2,)), DMA((2,)), DMA((2,)), DMA((8,)), DMA((8,)),
            DMA((4, 5)), DMA((4, 5)),
        ],
        compiler_params=pltpu.CompilerParams(
            collective_id=1, has_side_effects=True, vmem_limit_bytes=VMEM_LIMIT
        ),
    )(*args)
    return out.reshape(4, 2, 2, 8, 128)


def solution(mesh):
    placed = (
        P(None, None, None, "box", None),
        P(None, None, "dir", None),
        P(None, "box", None),
        P(None, None, "dir", None),
        P(None, None, None, "dir"),
        P(),
        P(),
        P(),
        P(),
        P(None, None, "dir"),
        P(None, None, "dir"),
        P(None, None, "dir"),
        P(None, None, None, "dir"),
        P(None, None, None, "dir"),
        P(None, None, None, "dir"),
        P(),
    )
    return jax.shard_map(
        shards,
        mesh=mesh,
        in_specs=placed,
        out_specs=P("dir", None, None, "box", None),
        check_vma=False,
    )
```

time: 112 us -> 62.7 us (0.56)
  the two profiles are of different devices: /device:TPU:103 before, /device:TPU:1 now
where the time goes in v2:
time: 62.7 us; the launch traced here: 62.4 us
  Pallas kernels  57.4 us (92%)
  local copies, waits for them, and re-layouts  4.98 us (8%)
    pallas_call x1, Pallas kernels, shards(): pl.pallas_call(functools.partial(whole, dirs, boxes), out_shape=jax.Shape...  57.4 us
    unnamed x7, local copies, waits for them, and re-layouts  2.82 us

profile of v2, /device:TPU:1, one launch (start us, length us, event | category | flops | bytes accessed | tf_op | source)
XLA Modules:
  0.0 62.4 jit_solution(3240982560501373959)
XLA Ops:
  0.0 1.2 %copy.22 = bf16[64,2,2,4,2,128]{5,3,1,0,4,2:T(4,128)(2,1)S(1)} copy(bf16[64,2,2,4,2,128]{5,4,3,2,1,0:T(2,128)(2,1)} %bitcast.22) | data formatting | bytes 1048576 | tf_op jit(solution)/shard_map/reshape | solution.py:537
  1.2 0.0 copy-start
  1.2 1.0 %reshape.19.source = bf16[2,2,128,512]{3,2,1,0:T(8,128)(2,1)} reshape(bf16[2,2,64,2,4,128]{5,4,3,2,1,0:T(4,128)(2,1)S(1)} %bitcast.21) | data formatting | bytes 1048576 | tf_op jit(solution)/shard_map/reshape | solution.py:538
  2.2 0.0 copy-done
  2.2 0.0 copy-start.1
  2.2 0.7 %copy.20.theta_two = f32[32,16]{1,0:T(8,128)} copy(f32[32,16]{0,1:T(8,128)S(1)} %copy-done) | data formatting | bytes 4096 | tf_op args[6]
  2.9 0.0 copy-done.1
  2.9 0.7 %copy.19.theta_one = f32[16,8]{1,0:T(8,128)} copy(f32[16,8]{0,1:T(8,128)S(1)} %copy-done.1) | data formatting | bytes 1024 | tf_op args[5]
  3.5 57.4 %shard_map.163 = f32[8,2,8,128]{3,2,1,0:T(8,128)} custom-call(bf16[2,2,128,512]{3,2,1,0:T(8,128)(2,1)} %reshape.19.source, bf16[216,64]{1,0:T(8,128)(2,1)} %bitcast.26, s32[27,8,128]{2,1,0:T(8,128)} %mask.1, bf16[2,8,64]{2,1,0:T(8,128)(2,1)} %bitcast.35, bf16[2,8,4,16]{3,2,1,0:T(4,128)(2,1)} %bitcast.30, f32[16,8]{1,0:T(8,128)} %copy.19.theta_one, ...), custom_call_target="tpu_custom_call" | custom-call | tf_op jit(solution)/shard_map/pallas_call | solution.py:550
  60.9 1.5 %copy.24 = f32[4,2,2,8,128]{4,3,2,1,0:T(8,128)} copy(f32[4,2,2,8,128]{4,3,2,1,0:T(8,128)} %bitcast.23) | data formatting | bytes 131072
Async XLA Ops:
  1.2 1.0 %copy-start = (f32[32,16]{0,1:T(8,128)S(1)}, f32[32,16]{0,1:T(8,128)}, u32[]{:S(2)}) copy-start(f32[32,16]{0,1:T(8,128)} %param.23) | copy-start | bytes 6148
  2.2 0.7 %copy-start.1 = (f32[16,8]{0,1:T(8,128)S(1)}, f32[16,8]{0,1:T(8,128)}, u32[]{:S(2)}) copy-start(f32[16,8]{0,1:T(8,128)} %param.22) | copy-start | bytes 1540

commit v3 on v2

--- a/solution.py
+++ b/solution.py
@@ -12,6 +12,7 @@
 F32 = jnp.float32
 BF16 = jnp.bfloat16
 VMEM_LIMIT = 56 * 1024 * 1024
+INPUTS = 17
 
 
 def iota(shape, dim):
@@ -57,7 +58,7 @@
         spread = onehot(
             iota((coarse_t, coarse_p * coarse_t), 1) % coarse_t == iota((coarse_t, coarse_p * coarse_t), 0)
         )
-        tiled = jnp.concatenate([dot_left(theta, spread)] * fine_p, axis=0)
+        tiled = jnp.concatenate([dot_left(theta, spread, ((0,), (0,)))] * fine_p, axis=0)
         fine_dim, coarse_dim = 0, 1
     p = iota(tiled.shape, fine_dim) // fine_t
     tap = iota(tiled.shape, coarse_dim) // coarse_t - first(p)
@@ -98,18 +99,20 @@
     )
 
 
-def whole(
-    dirs, boxes,
-    source, near_blocks, mask, radiate, receive, theta_one, theta_two, theta_two_t, theta_three_t, taps,
-    shift_one, shift_two, shift_three, trans_one, trans_two, trans_three, lists, shuffle,
-    out_ref,
-    message, gathered, rim_out, rims, leaf_halo, halo_one, halo_two, halo_three, one, two, three,
-    leaf, shape_high, shape_low, far_high, far_low, products, rolled, near,
-    table_one, table_two, table_three, ext_one, ext_two, ext_three,
-    partial, got_core, held, got_x, held_x, got_z,
-    send, receive_sem, rim_send, rim_receive, leaf_send, leaf_receive, halo_send, halo_receive,
-    sum_send, sum_receive,
-):
+def whole(dirs, boxes, *refs):
+    outside, out_ref, inside = refs[:INPUTS], refs[INPUTS], refs[INPUTS + 1 : 2 * INPUTS + 1]
+    (
+        leaf_rows, near_blocks, mask, radiate, receive, theta_one, theta_two, theta_three, taps,
+        shift_one, shift_two, shift_three, trans_one, trans_two, trans_three, lists, shuffle,
+    ) = inside
+    (
+        in_sem, wide_rows, source, message, gathered, rim_out, rims, leaf_halo, halo_one, halo_two, halo_three,
+        one, two, three, leaf, shape_high, shape_low, far_high, far_low, products, rolled, near,
+        table_one, table_two, table_three, ext_one, ext_two, ext_three,
+        partial, got_core, held, got_x, held_x, got_z,
+        send, receive_sem, rim_send, rim_receive, leaf_send, leaf_receive, halo_send, halo_receive,
+        sum_send, sum_receive,
+    ) = refs[2 * INPUTS + 1 :]
     me, box = lax.axis_index("dir"), lax.axis_index("box")
     has = {-1: box > 0, 1: box < boxes - 1, -2: box > 1, 2: box < boxes - 2}
     beside = {e: {"box": lax.rem(box + boxes + e, boxes)} for e in has}
@@ -125,6 +128,16 @@
             pl.semaphore_signal(barrier, inc=1, device_id=beside[e], device_id_type=MESH)
 
         count = count + jnp.where(has[e], 1, 0)
+
+    loads = [pltpu.make_async_copy(outside[i], inside[i], in_sem.at[i]) for i in range(INPUTS)]
+    early = (3, 4, 9, 10)
+    for i in early:
+        loads[i].start()
+    for i in range(INPUTS):
+        if i not in early:
+            loads[i].start()
+    for i in early:
+        loads[i].wait()
 
     taken = [receive[c, :, u, :].astype(F32) for c in range(2) for u in range(4)]
     lane = iota((64, 128), 1)
@@ -138,6 +151,9 @@
     rim_out[0] = jnp.concatenate([angles_one, angles_two[:, 96:], pad], axis=1)
     rim_out[1] = jnp.concatenate([angles_one, angles_two[:, :32], pad], axis=1)
 
+    for i in range(INPUTS):
+        if i not in early:
+            loads[i].wait()
     up_one = interpolation(
         taps, 0, theta_one[...], (6, 16), (5, 8), lambda p: p, lambda p: p // 2, False
     )
@@ -145,11 +161,16 @@
         taps, 1, theta_two[...], (6, 32), (6, 16), lambda p: p + 1, lambda p: (p + 1) // 2, False
     )
     back_two = interpolation(
-        taps, 1, theta_two_t[...], (6, 32), (6, 16), lambda p: p + 1, lambda p: (p + 1) // 2, True
+        taps, 1, theta_two[...], (6, 32), (6, 16), lambda p: p + 1, lambda p: (p + 1) // 2, True
     )
     up_three = interpolation(
-        taps, 2, theta_three_t[...], (8, 64), (6, 32), lambda p: p, lambda p: p // 2, True
-    )
+        taps, 2, theta_three[...], (8, 64), (6, 32), lambda p: p, lambda p: p // 2, True
+    )
+    wide_rows[...] = leaf_rows[...].astype(F32)
+    for r in range(2):
+        for x in range(8):
+            layer = wide_rows[pl.ds(8 * r + x, 128, stride=16), :].astype(BF16)
+            source[r, x % 2, :, 128 * (x // 2) : 128 * (x // 2) + 128] = layer
     for r in range(2):
         for ox in range(2):
             mixed = dot(source[r, ox], shuffle[...]).astype(BF16)
@@ -514,7 +535,7 @@
 
 
 VMEM = pl.BlockSpec(memory_space=pltpu.VMEM)
-SMEM = pl.BlockSpec(memory_space=pltpu.SMEM)
+HBM = pl.BlockSpec(memory_space=pltpu.HBM)
 DMA = pltpu.SemaphoreType.DMA
 
 
@@ -534,25 +555,25 @@
     shift_one, shift_two, shift_three, trans_one, trans_two, trans_three, far_lists,
 ):
     dirs, boxes = lax.axis_size("dir"), lax.axis_size("box")
-    layers = source.reshape(64, 2, 2, 4, 2, 128)
-    layers = jnp.transpose(layers, (2, 4, 0, 1, 3, 5)).reshape(2, 2, 128, 512)
     args = (
-        layers, near_blocks.reshape(216, 64), near_mask, radiate[:, :, 0], jnp.transpose(receive, (0, 1, 3, 2)),
-        theta_one, theta_two, theta_two.T, theta_three.T, phi_taps,
+        source.reshape(2048, 128), near_blocks.reshape(216, 64), near_mask, radiate[:, :, 0], jnp.transpose(receive, (0, 1, 3, 2)),
+        theta_one.T, theta_two.T, theta_three.T, phi_taps,
         jnp.transpose(shift_one, (0, 2, 1)), jnp.transpose(shift_two, (0, 2, 1)),
         jnp.transpose(shift_three, (0, 2, 1)), jnp.transpose(trans_one, (1, 2, 3, 0)),
         jnp.transpose(trans_two, (0, 1, 3, 2)).reshape(64, 4, 32),
         jnp.transpose(trans_three, (0, 1, 3, 2)).reshape(64, 8, 64),
         jnp.transpose(far_lists, (0, 2, 1)), jnp.asarray(shuffle_table(), BF16),
     )
-    specs = [VMEM] * len(args)
-    specs[16] = SMEM
+    copies = [pltpu.VMEM(a.shape, a.dtype) for a in args]
+    copies[15] = pltpu.SMEM(args[15].shape, args[15].dtype)
     out = pl.pallas_call(
         functools.partial(whole, dirs, boxes),
         out_shape=jax.ShapeDtypeStruct((8, 2, 8, 128), F32),
-        in_specs=specs,
+        in_specs=[HBM] * INPUTS,
         out_specs=VMEM,
-        scratch_shapes=[
+        scratch_shapes=copies
+        + [
+            DMA((INPUTS,)), held_in(2048, 128), held_in(2, 2, 128, 512, dtype=BF16),
             held_in(16, 128, dtype=BF16), held_in(16, 16, 128, dtype=BF16), held_in(2, 8, 128), held_in(2, 8, 128),
             held_in(2, 2, 128, 128, dtype=BF16), held_in(2, 64, 128), held_in(2, 16, 512), held_in(4, 8, 512),
             held_in(128, 128), held_in(16, 512), held_in(8, 512),

time: 62.7 us -> 56.7 us (0.904)
  the two profiles are of different devices: /device:TPU:1 before, /device:TPU:32 now
where the time goes in v3:
time: 56.7 us; the launch traced here: 56.2 us
  Pallas kernels  54.8 us (97%)
  local copies, waits for them, and re-layouts  1.47 us (3%)
    pallas_call x1, Pallas kernels, shards(): pl.pallas_call(functools.partial(whole, dirs, boxes), out_shape=jax.Shape...  54.8 us
    unnamed x1, local copies, waits for them, and re-layouts  1.47 us

profile of v3, /device:TPU:32, one launch (start us, length us, event | category | flops | bytes accessed | tf_op | source)
XLA Modules:
  0.0 56.2 jit_solution(18200288029589281640)
XLA Ops:
  0.0 54.8 %shard_map.163 = f32[8,2,8,128]{3,2,1,0:T(8,128)} custom-call(bf16[2048,128]{1,0:T(8,128)(2,1)} %bitcast.19, bf16[216,64]{1,0:T(8,128)(2,1)} %bitcast.23, s32[27,8,128]{2,1,0:T(8,128)} %refs_2_.1, bf16[2,8,64]{2,1,0:T(8,128)(2,1)} %bitcast.32, bf16[2,8,4,16]{3,2,1,0:T(4,128)(2,1)} %bitcast.26, f32[8,16]{1,0:T(8,128)} %bitcast.33, f32[16,32]{1,0:T(8,128)} %bitcast.29, ...), custom_call_target="tpu_custom_call" | custom-call | tf_op jit(solution)/shard_map/pallas_call | solution.py:569
  54.8 1.5 %copy.19 = f32[4,2,2,8,128]{4,3,2,1,0:T(8,128)} copy(f32[4,2,2,8,128]{4,3,2,1,0:T(8,128)} %bitcast.20) | data formatting | bytes 131072

commit v4 on v3

--- a/solution.py
+++ b/solution.py
@@ -109,19 +109,25 @@
         in_sem, wide_rows, source, message, gathered, rim_out, rims, leaf_halo, halo_one, halo_two, halo_three,
         one, two, three, leaf, shape_high, shape_low, far_high, far_low, products, rolled, near,
         table_one, table_two, table_three, ext_one, ext_two, ext_three,
-        partial, got_core, held, got_x, held_x, got_z,
+        partial, got_core, held, coded, got_coded,
         send, receive_sem, rim_send, rim_receive, leaf_send, leaf_receive, halo_send, halo_receive,
         sum_send, sum_receive,
     ) = refs[2 * INPUTS + 1 :]
     me, box = lax.axis_index("dir"), lax.axis_index("box")
     has = {-1: box > 0, 1: box < boxes - 1, -2: box > 1, 2: box < boxes - 2}
     beside = {e: {"box": lax.rem(box + boxes + e, boxes)} for e in has}
-    peers = {e: {"dir": lax.rem(me + e, dirs)} for e in range(1, dirs)}
+    place_x, place_z, core = me // 4, me // 2 % 2, me % 2
+    places = [(dx, dz, dc) for dz in (1, 0) for dx in (2, 1, 3, 0) for dc in (1, 0)][: dirs - 1]
+    number = {p: 4 * lax.rem(place_x + p[0], 4) + 2 * ((place_z + p[1]) % 2) + (core + p[2]) % 2 for p in places}
+    peers = {p: {"dir": number[p]} for p in places}
+    slot = {p: 4 * p[0] + 2 * p[1] + p[2] for p in places}
+    back = {p: slot[((4 - p[0]) % 4, p[1], p[2])] for p in places}
+    after, before = {"dir": lax.rem(me + 1, dirs)}, {"dir": lax.rem(me + dirs - 1, dirs)}
 
     barrier = pltpu.get_barrier_semaphore()
     count = dirs - 1
-    for e in range(1, dirs):
-        pl.semaphore_signal(barrier, inc=1, device_id=peers[e], device_id_type=MESH)
+    for p in places:
+        pl.semaphore_signal(barrier, inc=1, device_id=peers[p], device_id_type=MESH)
     for e in has:
         @pl.when(has[e])
         def _(e=e):
@@ -205,19 +211,19 @@
             leaf_halo[side] = jnp.zeros((2, 128, 128), BF16)
             halo_one[side] = jnp.zeros((64, 128), F32)
             halo_two[side] = jnp.zeros((16, 512), F32)
-    for slot, e in enumerate((-2, -1, 1, 2)):
+    for layer, e in enumerate((-2, -1, 1, 2)):
         @pl.when(jnp.logical_not(has[e]))
-        def _(slot=slot):
-            halo_three[slot] = jnp.zeros((8, 512), F32)
+        def _(layer=layer):
+            halo_three[layer] = jnp.zeros((8, 512), F32)
 
     pl.semaphore_wait(barrier, count)
     table_copies = [
-        remote(rim_out.at[0], rims.at[0], rim_send.at[0], rim_receive.at[0], peers[1]),
-        remote(rim_out.at[1], rims.at[1], rim_send.at[1], rim_receive.at[1], peers[dirs - 1]),
+        remote(rim_out.at[0], rims.at[0], rim_send.at[0], rim_receive.at[0], after),
+        remote(rim_out.at[1], rims.at[1], rim_send.at[1], rim_receive.at[1], before),
     ]
-    for e in range(1, dirs):
+    for p in places:
         table_copies.append(
-            remote(message, gathered.at[dirs - e], send.at[e], receive_sem.at[dirs - e], peers[e])
+            remote(message, gathered.at[back[p]], send.at[back[p]], receive_sem.at[back[p]], peers[p])
         )
     for copy in table_copies:
         copy.start()
@@ -278,8 +284,12 @@
     pad = jnp.zeros((8, 32), F32)
     angles = jnp.concatenate([rims[0, :, 0:32], angles_one, rims[1, :, 0:32], pad], axis=1)
     turns = cosines(angles).T
-    tables = gathered[...].astype(F32)
-    sources = jnp.concatenate([tables[(a - 2) % 16, 8:16] for a in range(5)], axis=0)
+    sources = []
+    for a in range(5):
+        owner = lax.rem(me + dirs - 2 + a, dirs)
+        at = 4 * lax.rem(owner // 4 + 4 - place_x, 4) + 2 * ((owner // 2 + place_z) % 2) + (owner + core) % 2
+        sources.append(gathered[at].astype(F32)[8:16])
+    sources = jnp.concatenate(sources, axis=0)
     send_real = dot_left(up_one, sources.astype(BF16))
     send_turned = turned(send_real)
     even = iota((96, 128), 1) % 2 == 0
@@ -349,15 +359,16 @@
     for e, copy in halo_copies[4:]:
         pl.when(has[e])(copy.start)
 
+    tables = gathered[...].astype(F32)
     stacked = jnp.concatenate([tables[e, 0:8] for e in range(16)], axis=0)
     row, lane = iota((128, 640), 0), iota((128, 640), 1)
     azimuth = (me + 14 + lane // 128) % 16
     pick = onehot(row == 64 * (lane % 2) + 16 * (lane % 8 // 2) + azimuth)
-    sender = (row // 8 + me) % 16
-    placed = jnp.where(lane % 128 // 8 == sender, dot(stacked.astype(BF16), pick), 0.0)
-    summed = placed[0:8]
-    for e in range(1, 16):
-        summed = summed + placed[8 * e : 8 * e + 8]
+    placed = dot(stacked.astype(BF16), pick)
+    owner = iota((8, 640), 1) % 128 // 8
+    summed = jnp.where(owner == me, placed[0:8], 0.0)
+    for p in places:
+        summed = jnp.where(owner == number[p], placed[8 * slot[p] : 8 * slot[p] + 8], summed)
     targets = jnp.concatenate([summed[:, 128 * a : 128 * a + 128] for a in range(5)], axis=0)
     take_real = dot_left(up_one, targets.astype(BF16))
     take_turned = turned(take_real)
@@ -457,34 +468,21 @@
         level_one.append(dot3(back_two, value) + jnp.concatenate([pad, field, pad], axis=0))
     high, low = split(jnp.concatenate(level_one, axis=0))
 
-    x, z, core = me // 4, me // 2 % 2, me % 2
-    sibling = {"dir": me + 1 - 2 * core}
-    across = {"dir": me + 2 - 4 * z}
-    others = [peers[4 * e] for e in range(1, 4)]
+    sibling = peers[(0, 0, 1)]
     to_core = [
-        remote(partial.at[i, 1 - core], got_core.at[i], sum_send.at[i, 0], sum_receive.at[i, 0], sibling)
+        remote(partial.at[i, 1 - core], got_core.at[i], sum_send.at[i], sum_receive.at[i], sibling)
         for i in range(4)
     ]
-    to_x = [
-        [
-            remote(
-                held.at[i, lax.rem(x + e, 4)], got_x.at[i, 3 - e], sum_send.at[i, e], sum_receive.at[i, 4 - e],
-                others[e - 1],
-            )
-            for e in range(1, 4)
-        ]
-        for i in range(4)
-    ]
-    to_z = [
-        remote(held_x.at[i, 1 - z], got_z.at[i], sum_send.at[i, 4], sum_receive.at[i, 4], across)
-        for i in range(4)
+    owners = [p for p in places if p[2] == 0]
+    to_owner = [
+        remote(coded.at[j], got_coded.at[owners.index(((4 - p[0]) % 4, p[1], 0))], sum_send.at[4 + j],
+               sum_receive.at[4 + owners.index(((4 - p[0]) % 4, p[1], 0))], peers[p])
+        for j, p in enumerate(owners)
     ]
 
     def after_core(i):
         to_core[i].wait_recv()
-        held[i] = partial[i, core] + got_core[i]
-        for copy in to_x[i]:
-            copy.start()
+        held[:, :, 16 * i : 16 * i + 16, :] = partial[i, core] + got_core[i]
 
     for i in range(4):
         for o in (2 * i, 2 * i + 1):
@@ -498,28 +496,30 @@
         if i > 0:
             after_core(i - 1)
     after_core(3)
-    for i in range(4):
-        for copy in to_x[i]:
-            copy.wait_recv()
-        held_x[i] = held[i, x] + (got_x[i, 0] + got_x[i, 1] + got_x[i, 2])
-        to_z[i].start()
+    for j, p in enumerate(owners):
+        block = held[lax.rem(place_x + p[0], 4), (place_z + p[1]) % 2]
+        largest = jnp.max(jnp.abs(block), axis=0, keepdims=True)
+        power = jnp.ceil(jnp.log2(jnp.maximum(largest, 1e-25)))
+        values = jnp.floor(block * (32000.0 / jnp.exp2(power)) + 0.5)
+        coded[j, 0:64] = values.astype(jnp.int32).astype(jnp.int16)
+        coded[j, 64:80] = jnp.broadcast_to(power, (16, 256)).astype(jnp.int32).astype(jnp.int16)
+        to_owner[j].start()
     for e, copy in halo_copies:
         pl.when(has[e])(copy.wait_send)
-    for i in range(4):
-        to_core[i].wait_send()
-        for copy in to_x[i]:
-            copy.wait_send()
-    far = []
-    for i in range(4):
-        to_z[i].wait_recv()
-        far.append(held_x[i, z] + got_z[i])
-    for i in range(4):
-        to_z[i].wait_send()
+    for copy in to_core + to_owner:
+        copy.wait_send()
+    far = held[place_x, place_z]
+    for copy in to_owner:
+        copy.wait_recv()
+    for j in range(len(owners)):
+        power = got_coded[j, 64:80].astype(jnp.int32).astype(F32)[0:1]
+        values = got_coded[j, 0:64].astype(jnp.int32).astype(F32)
+        far = far + values * (jnp.exp2(power) / 32000.0)
     rows = []
     for r in range(2):
         for ox in range(2):
             pieces = [
-                far[2 * ox + o // 2][8 * (o % 2) : 8 * (o % 2) + 8, 128 * r : 128 * r + 128] for o in range(4)
+                far[32 * ox + 8 * o : 32 * ox + 8 * o + 8, 128 * r : 128 * r + 128] for o in range(4)
             ]
             rows.append(jnp.concatenate(pieces, axis=1))
     high, low = split(jnp.concatenate(rows, axis=0))
@@ -582,10 +582,10 @@
             held_in(2, 10, 216, 128), held_in(27, 8, 128), held_in(2, 8, 8, 128),
             held_in(2, 32, 128), held_in(64, 128), held_in(64, 512),
             held_in(5, 8, 8, 8, 128), held_in(25, 6, 8, 512), held_in(4, 5, 8, 512),
-            held_in(4, 2, 4, 2, 16, 256), held_in(4, 4, 2, 16, 256), held_in(4, 4, 2, 16, 256),
-            held_in(4, 3, 2, 16, 256), held_in(4, 2, 16, 256), held_in(4, 16, 256),
+            held_in(4, 2, 4, 2, 16, 256), held_in(4, 4, 2, 16, 256), held_in(4, 2, 64, 256),
+            held_in(7, 80, 256, dtype=jnp.int16), held_in(7, 80, 256, dtype=jnp.int16),
             DMA((16,)), DMA((16,)), DMA((2,)), DMA((2,)), DMA((2,)), DMA((2,)), DMA((8,)), DMA((8,)),
-            DMA((4, 5)), DMA((4, 5)),
+            DMA((11,)), DMA((11,)),
         ],
         compiler_params=pltpu.CompilerParams(
             collective_id=1, has_side_effects=True, vmem_limit_bytes=VMEM_LIMIT

time: 56.7 us -> 59.3 us (1.046)
  the two profiles are of different devices: /device:TPU:32 before, /device:TPU:96 now
where the time goes in v4:
time: 59.3 us; the launch traced here: 59.2 us
  Pallas kernels  57.7 us (97%)
  local copies, waits for them, and re-layouts  1.47 us (2%)
    pallas_call x1, Pallas kernels, shards(): pl.pallas_call(functools.partial(whole, dirs, boxes), out_shape=jax.Shape...  57.7 us
    unnamed x1, local copies, waits for them, and re-layouts  1.47 us

profile of v4, /device:TPU:96, one launch (start us, length us, event | category | flops | bytes accessed | tf_op | source)
XLA Modules:
  0.0 59.2 jit_solution(250904753747820791)
XLA Ops:
  0.0 57.7 %shard_map.163 = f32[8,2,8,128]{3,2,1,0:T(8,128)} custom-call(bf16[2048,128]{1,0:T(8,128)(2,1)} %bitcast.19, bf16[216,64]{1,0:T(8,128)(2,1)} %bitcast.23, s32[27,8,128]{2,1,0:T(8,128)} %refs_2_.1, bf16[2,8,64]{2,1,0:T(8,128)(2,1)} %bitcast.32, bf16[2,8,4,16]{3,2,1,0:T(4,128)(2,1)} %bitcast.26, f32[8,16]{1,0:T(8,128)} %bitcast.33, f32[16,32]{1,0:T(8,128)} %bitcast.29, ...), custom_call_target="tpu_custom_call" | custom-call | tf_op jit(solution)/shard_map/pallas_call | solution.py:569
  57.7 1.5 %copy.19 = f32[4,2,2,8,128]{4,3,2,1,0:T(8,128)} copy(f32[4,2,2,8,128]{4,3,2,1,0:T(8,128)} %bitcast.20) | data formatting | bytes 131072

commit v5 on v4

--- a/solution.py
+++ b/solution.py
@@ -473,12 +473,28 @@
         remote(partial.at[i, 1 - core], got_core.at[i], sum_send.at[i], sum_receive.at[i], sibling)
         for i in range(4)
     ]
-    owners = [p for p in places if p[2] == 0]
-    to_owner = [
-        remote(coded.at[j], got_coded.at[owners.index(((4 - p[0]) % 4, p[1], 0))], sum_send.at[4 + j],
-               sum_receive.at[4 + owners.index(((4 - p[0]) % 4, p[1], 0))], peers[p])
-        for j, p in enumerate(owners)
-    ]
+    across = peers[(0, 1, 0)]
+    along = (2, 1, 3)
+    to_x = []
+    for part in range(2):
+        for j, e in enumerate(along):
+            there = 3 * part + along.index(4 - e)
+            to_x.append(remote(
+                coded.at[3 * part + j], got_coded.at[there], sum_send.at[4 + there], sum_receive.at[4 + there],
+                peers[(e, 0, 0)],
+            ))
+    to_z = remote(coded.at[6], got_coded.at[6], sum_send.at[10], sum_receive.at[10], across)
+
+    def encode(j, block):
+        largest = jnp.max(jnp.abs(block), axis=0, keepdims=True)
+        power = jnp.ceil(jnp.log2(jnp.maximum(largest, 1e-25)))
+        values = jnp.floor(block * (32000.0 / jnp.exp2(power)) + 0.5)
+        coded[j, 0:64] = values.astype(jnp.int32).astype(jnp.int16)
+        coded[j, 64:80] = jnp.broadcast_to(power, (16, 256)).astype(jnp.int32).astype(jnp.int16)
+
+    def decode(j):
+        power = got_coded[j, 64:80].astype(jnp.int32).astype(F32)[0:1]
+        return got_coded[j, 0:64].astype(jnp.int32).astype(F32) * (jnp.exp2(power) / 32000.0)
 
     def after_core(i):
         to_core[i].wait_recv()
@@ -496,25 +512,24 @@
         if i > 0:
             after_core(i - 1)
     after_core(3)
-    for j, p in enumerate(owners):
-        block = held[lax.rem(place_x + p[0], 4), (place_z + p[1]) % 2]
-        largest = jnp.max(jnp.abs(block), axis=0, keepdims=True)
-        power = jnp.ceil(jnp.log2(jnp.maximum(largest, 1e-25)))
-        values = jnp.floor(block * (32000.0 / jnp.exp2(power)) + 0.5)
-        coded[j, 0:64] = values.astype(jnp.int32).astype(jnp.int16)
-        coded[j, 64:80] = jnp.broadcast_to(power, (16, 256)).astype(jnp.int32).astype(jnp.int16)
-        to_owner[j].start()
+    for part in range(2):
+        half = 1 - place_z if part == 0 else place_z
+        for j, e in enumerate(along):
+            encode(3 * part + j, held[lax.rem(place_x + e, 4), half])
+            to_x[3 * part + j].start()
+    for copy in to_x[:3]:
+        copy.wait_recv()
+    encode(6, held[place_x, 1 - place_z] + (decode(0) + decode(1) + decode(2)))
+    to_z.start()
+    for copy in to_x[3:]:
+        copy.wait_recv()
+    far = held[place_x, place_z] + (decode(3) + decode(4) + decode(5))
     for e, copy in halo_copies:
         pl.when(has[e])(copy.wait_send)
-    for copy in to_core + to_owner:
+    for copy in to_core + to_x:
         copy.wait_send()
-    far = held[place_x, place_z]
-    for copy in to_owner:
-        copy.wait_recv()
-    for j in range(len(owners)):
-        power = got_coded[j, 64:80].astype(jnp.int32).astype(F32)[0:1]
-        values = got_coded[j, 0:64].astype(jnp.int32).astype(F32)
-        far = far + values * (jnp.exp2(power) / 32000.0)
+    to_z.wait()
+    far = far + decode(6)
     rows = []
     for r in range(2):
         for ox in range(2):

time: 59.3 us -> 53.7 us (0.906)
  the two profiles are of different devices: /device:TPU:96 before, /device:TPU:32 now
where the time goes in v5:
time: 53.7 us; the launch traced here: 53.5 us
  Pallas kernels  52 us (97%)
  local copies, waits for them, and re-layouts  1.47 us (3%)
    pallas_call x1, Pallas kernels, shards(): pl.pallas_call(functools.partial(whole, dirs, boxes), out_shape=jax.Shape...  52 us
    unnamed x1, local copies, waits for them, and re-layouts  1.47 us

profile of v5, /device:TPU:32, one launch (start us, length us, event | category | flops | bytes accessed | tf_op | source)
XLA Modules:
  0.0 53.5 jit_solution(4465649082967336789)
XLA Ops:
  0.0 52.0 %shard_map.163 = f32[8,2,8,128]{3,2,1,0:T(8,128)} custom-call(bf16[2048,128]{1,0:T(8,128)(2,1)} %bitcast.19, bf16[216,64]{1,0:T(8,128)(2,1)} %bitcast.23, s32[27,8,128]{2,1,0:T(8,128)} %refs_2_.1, bf16[2,8,64]{2,1,0:T(8,128)(2,1)} %bitcast.32, bf16[2,8,4,16]{3,2,1,0:T(4,128)(2,1)} %bitcast.26, f32[8,16]{1,0:T(8,128)} %bitcast.33, f32[16,32]{1,0:T(8,128)} %bitcast.29, ...), custom_call_target="tpu_custom_call" | custom-call | tf_op jit(solution)/shard_map/pallas_call | solution.py:584
  52.0 1.5 %copy.19 = f32[4,2,2,8,128]{4,3,2,1,0:T(8,128)} copy(f32[4,2,2,8,128]{4,3,2,1,0:T(8,128)} %bitcast.20) | data formatting | bytes 131072

commit v6 on v5

--- a/solution.py
+++ b/solution.py
@@ -227,17 +227,6 @@
         )
     for copy in table_copies:
         copy.start()
-    leaf_copies = [
-        (1, remote(
-            source.at[:, 1, :, pl.ds(384, 128)], leaf_halo.at[0], leaf_send.at[0], leaf_receive.at[0], beside[1]
-        )),
-        (-1, remote(
-            source.at[:, 0, :, pl.ds(0, 128)], leaf_halo.at[1], leaf_send.at[1], leaf_receive.at[1], beside[-1]
-        )),
-    ]
-    for e, copy in leaf_copies:
-        pl.when(has[e])(copy.start)
-
     lane = iota((64, 128), 1)
     double = dot(near_blocks[...], onehot(lane // 2 == iota((64, 128), 0))).astype(BF16)
     row, column = iota((216, 216), 0), iota((216, 216), 1)
@@ -259,24 +248,6 @@
             layers = dot(blocks, source[r, ox])
             for x in range(4):
                 products[r, 1 + 2 * x + ox] = layers[:, 128 * x : 128 * x + 128]
-    for e, copy in leaf_copies:
-        pl.when(has[e])(copy.wait_send)
-        pl.when(has[-e])(copy.wait_recv)
-    for r in range(2):
-        for side in range(2):
-            products[r, 9 * side] = dot(blocks, leaf_halo[side, r])
-    for r in range(2):
-        for x in range(8):
-            total = jnp.zeros((8, 128), F32)
-            for inner in range(9):
-                dy, dz = inner // 3 - 1, inner % 3 - 1
-                term = jnp.zeros((8, 128), F32)
-                for dx in range(3):
-                    k = 9 * dx + inner
-                    term = term + products[r, x + dx, 8 * k : 8 * k + 8, :] * rolled[k, x : x + 1, :]
-                total = total + pltpu.roll(term, (-16 * dy - dz) % 128, 1)
-            near[r, x] = total
-
     for copy in table_copies:
         copy.wait_send()
     for copy in table_copies:
@@ -357,6 +328,17 @@
     together = onehot(row // 16 * 2 + row // 2 % 2 == iota((8, 64), 0))
     three[...] = dot_right(together, jnp.concatenate(parts, axis=0))
     for e, copy in halo_copies[4:]:
+        pl.when(has[e])(copy.start)
+
+    leaf_copies = [
+        (1, remote(
+            source.at[:, 1, :, pl.ds(384, 128)], leaf_halo.at[0], leaf_send.at[0], leaf_receive.at[0], beside[1]
+        )),
+        (-1, remote(
+            source.at[:, 0, :, pl.ds(0, 128)], leaf_halo.at[1], leaf_send.at[1], leaf_receive.at[1], beside[-1]
+        )),
+    ]
+    for e, copy in leaf_copies:
         pl.when(has[e])(copy.start)
 
     tables = gathered[...].astype(F32)
@@ -512,15 +494,35 @@
         if i > 0:
             after_core(i - 1)
     after_core(3)
-    for part in range(2):
-        half = 1 - place_z if part == 0 else place_z
-        for j, e in enumerate(along):
-            encode(3 * part + j, held[lax.rem(place_x + e, 4), half])
-            to_x[3 * part + j].start()
+    for j, e in enumerate(along):
+        encode(j, held[lax.rem(place_x + e, 4), 1 - place_z])
+        to_x[j].start()
+    for j, e in enumerate(along):
+        encode(3 + j, held[lax.rem(place_x + e, 4), place_z])
     for copy in to_x[:3]:
         copy.wait_recv()
     encode(6, held[place_x, 1 - place_z] + (decode(0) + decode(1) + decode(2)))
     to_z.start()
+    for copy in to_x[3:]:
+        copy.start()
+
+    for e, copy in leaf_copies:
+        pl.when(has[e])(copy.wait_send)
+        pl.when(has[-e])(copy.wait_recv)
+    for r in range(2):
+        for side in range(2):
+            products[r, 9 * side] = dot(blocks, leaf_halo[side, r])
+    for r in range(2):
+        for x in range(8):
+            total = jnp.zeros((8, 128), F32)
+            for inner in range(9):
+                dy, dz = inner // 3 - 1, inner % 3 - 1
+                term = jnp.zeros((8, 128), F32)
+                for dx in range(3):
+                    k = 9 * dx + inner
+                    term = term + products[r, x + dx, 8 * k : 8 * k + 8, :] * rolled[k, x : x + 1, :]
+                total = total + pltpu.roll(term, (-16 * dy - dz) % 128, 1)
+            near[r, x] = total
     for copy in to_x[3:]:
         copy.wait_recv()
     far = held[place_x, place_z] + (decode(3) + decode(4) + decode(5))

time: 53.7 us -> 53.9 us (level)
  no operation moved by 1% of the time
where the time goes in v6:
time: 53.9 us; the launch traced here: 53.7 us
  Pallas kernels  52.2 us (97%)
  local copies, waits for them, and re-layouts  1.47 us (3%)
    pallas_call x1, Pallas kernels, shards(): pl.pallas_call(functools.partial(whole, dirs, boxes), out_shape=jax.Shape...  52.2 us
    unnamed x1, local copies, waits for them, and re-layouts  1.47 us

profile of v6, /device:TPU:32, one launch (start us, length us, event | category | flops | bytes accessed | tf_op | source)
XLA Modules:
  0.0 53.7 jit_solution(5188235768951549319)
XLA Ops:
  0.0 52.2 %shard_map.163 = f32[8,2,8,128]{3,2,1,0:T(8,128)} custom-call(bf16[2048,128]{1,0:T(8,128)(2,1)} %bitcast.19, bf16[216,64]{1,0:T(8,128)(2,1)} %bitcast.23, s32[27,8,128]{2,1,0:T(8,128)} %refs_2_.1, bf16[2,8,64]{2,1,0:T(8,128)(2,1)} %bitcast.32, bf16[2,8,4,16]{3,2,1,0:T(4,128)(2,1)} %bitcast.26, f32[8,16]{1,0:T(8,128)} %bitcast.33, f32[16,32]{1,0:T(8,128)} %bitcast.29, ...), custom_call_target="tpu_custom_call" | custom-call | tf_op jit(solution)/shard_map/pallas_call | solution.py:586
  52.2 1.5 %copy.19 = f32[4,2,2,8,128]{4,3,2,1,0:T(8,128)} copy(f32[4,2,2,8,128]{4,3,2,1,0:T(8,128)} %bitcast.20) | data formatting | bytes 131072

commit v7 on v6

--- a/solution.py
+++ b/solution.py
@@ -100,7 +100,8 @@
 
 
 def whole(dirs, boxes, *refs):
-    outside, out_ref, inside = refs[:INPUTS], refs[INPUTS], refs[INPUTS + 1 : 2 * INPUTS + 1]
+    outside, inside = refs[:INPUTS], refs[INPUTS + 2 : 2 * INPUTS + 2]
+    far_ref, near_ref = refs[INPUTS], refs[INPUTS + 1]
     (
         leaf_rows, near_blocks, mask, radiate, receive, theta_one, theta_two, theta_three, taps,
         shift_one, shift_two, shift_three, trans_one, trans_two, trans_three, lists, shuffle,
@@ -111,8 +112,8 @@
         table_one, table_two, table_three, ext_one, ext_two, ext_three,
         partial, got_core, held, coded, got_coded,
         send, receive_sem, rim_send, rim_receive, leaf_send, leaf_receive, halo_send, halo_receive,
-        sum_send, sum_receive,
-    ) = refs[2 * INPUTS + 1 :]
+        sum_send, sum_receive, near_sem,
+    ) = refs[2 * INPUTS + 2 :]
     me, box = lax.axis_index("dir"), lax.axis_index("box")
     has = {-1: box > 0, 1: box < boxes - 1, -2: box > 1, 2: box < boxes - 2}
     beside = {e: {"box": lax.rem(box + boxes + e, boxes)} for e in has}
@@ -522,7 +523,9 @@
                     k = 9 * dx + inner
                     term = term + products[r, x + dx, 8 * k : 8 * k + 8, :] * rolled[k, x : x + 1, :]
                 total = total + pltpu.roll(term, (-16 * dy - dz) % 128, 1)
-            near[r, x] = total
+            near[:, r, x, :] = total
+    near_copy = pltpu.make_async_copy(near, near_ref, near_sem)
+    near_copy.start()
     for copy in to_x[3:]:
         copy.wait_recv()
     far = held[place_x, place_z] + (decode(3) + decode(4) + decode(5))
@@ -546,9 +549,8 @@
         for ox in range(2):
             for x in range(4):
                 row = 8 * (2 * r + ox)
-                out_ref[:, r, 2 * x + ox, :] = (
-                    near[r, 2 * x + ox] + far[row : row + 8, 128 * x : 128 * x + 128]
-                )
+                far_ref[:, r, 2 * x + ox, :] = far[row : row + 8, 128 * x : 128 * x + 128]
+    near_copy.wait()
 
 
 VMEM = pl.BlockSpec(memory_space=pltpu.VMEM)
@@ -583,11 +585,11 @@
     )
     copies = [pltpu.VMEM(a.shape, a.dtype) for a in args]
     copies[15] = pltpu.SMEM(args[15].shape, args[15].dtype)
-    out = pl.pallas_call(
+    far, near = pl.pallas_call(
         functools.partial(whole, dirs, boxes),
-        out_shape=jax.ShapeDtypeStruct((8, 2, 8, 128), F32),
+        out_shape=[jax.ShapeDtypeStruct((8, 2, 8, 128), F32)] * 2,
         in_specs=[HBM] * INPUTS,
-        out_specs=VMEM,
+        out_specs=[VMEM, HBM],
         scratch_shapes=copies
         + [
             DMA((INPUTS,)), held_in(2048, 128), held_in(2, 2, 128, 512, dtype=BF16),
@@ -596,19 +598,19 @@
             held_in(128, 128), held_in(16, 512), held_in(8, 512),
             held_in(1024, 256, dtype=BF16), held_in(192, 1024, dtype=BF16), held_in(192, 1024, dtype=BF16),
             held_in(1024, 192, dtype=BF16), held_in(1024, 192, dtype=BF16),
-            held_in(2, 10, 216, 128), held_in(27, 8, 128), held_in(2, 8, 8, 128),
+            held_in(2, 10, 216, 128), held_in(27, 8, 128), held_in(8, 2, 8, 128),
             held_in(2, 32, 128), held_in(64, 128), held_in(64, 512),
             held_in(5, 8, 8, 8, 128), held_in(25, 6, 8, 512), held_in(4, 5, 8, 512),
             held_in(4, 2, 4, 2, 16, 256), held_in(4, 4, 2, 16, 256), held_in(4, 2, 64, 256),
             held_in(7, 80, 256, dtype=jnp.int16), held_in(7, 80, 256, dtype=jnp.int16),
             DMA((16,)), DMA((16,)), DMA((2,)), DMA((2,)), DMA((2,)), DMA((2,)), DMA((8,)), DMA((8,)),
-            DMA((11,)), DMA((11,)),
+            DMA((11,)), DMA((11,)), DMA,
         ],
         compiler_params=pltpu.CompilerParams(
             collective_id=1, has_side_effects=True, vmem_limit_bytes=VMEM_LIMIT
         ),
     )(*args)
-    return out.reshape(4, 2, 2, 8, 128)
+    return (far + near).reshape(4, 2, 2, 8, 128)
 
 
 def solution(mesh):

time: 53.9 us -> 53.9 us (level)
  other arithmetic: 0 us -> 1.51 us
  local copies, waits for them, and re-layouts: 1.47 us -> 0 us
    add x0 -> x1, other arithmetic: none -> 1.51 us  [shards(): return (far + near).reshape(4, 2, 2, 8, 128)]
    unnamed x1 -> x0, local copies, waits for them, and re-layouts: 1.47 us -> none
where the time goes in v7:
time: 53.9 us; the launch traced here: 53.7 us
  Pallas kernels  52.2 us (97%)
  other arithmetic  1.51 us (3%)
    pallas_call x1, Pallas kernels, shards(): pl.pallas_call(functools.partial(whole, dirs, boxes), out_shape=[jax.Shap...  52.2 us
    add x1, other arithmetic, shards(): return (far + near).reshape(4, 2, 2, 8, 128)  1.51 us

profile of v7, /device:TPU:32, one launch (start us, length us, event | category | flops | bytes accessed | tf_op | source)
XLA Modules:
  0.0 53.7 jit_solution(12488563674178204082)
XLA Ops:
  0.0 52.2 %shard_map.163 = (f32[8,2,8,128]{3,2,1,0:T(8,128)}, f32[8,2,8,128]{3,2,1,0:T(8,128)}) custom-call(bf16[2048,128]{1,0:T(8,128)(2,1)} %bitcast.19, bf16[216,64]{1,0:T(8,128)(2,1)} %bitcast.22, s32[27,8,128]{2,1,0:T(8,128)} %refs_2_.1, bf16[2,8,64]{2,1,0:T(8,128)(2,1)} %bitcast.31, bf16[2,8,4,16]{3,2,1,0:T(4,128)(2,1)} %bitcast.25, f32[8,16]{1,0:T(8,128)} %bitcast.32, ...), custom_call_target="tpu_custom_call" | custom-call | tf_op jit(solution)/shard_map/pallas_call | solution.py:588
  52.2 1.5 %add.3 = f32[8,2,8,128]{3,2,1,0:T(8,128)} add(f32[8,2,8,128]{3,2,1,0:T(8,128)} %get-tuple-element.7, f32[8,2,8,128]{3,2,1,0:T(8,128)} %get-tuple-element.8) | non-fusion elementwise | flops 16384 | bytes 196608 | tf_op jit(solution)/shard_map/add | solution.py:613

commit v8 on v6

--- a/solution.py
+++ b/solution.py
@@ -193,6 +193,11 @@
             place = onehot(iota((16, 128), 1) % 32 == 16 * a + iota((16, 128), 0))
             total = total + dot_left(trans_one[c, :, a, :], place, ((0,), (0,)))
         table_one[c] = total
+    turns_three = cosines(jnp.concatenate([shift_three[:, a, :] for a in range(8)], axis=1))
+    row, column = iota((16, 8), 0), iota((16, 8), 1)
+    expand = onehot(column == 4 * (row // 8) + 2 * (row // 4 % 2) + row % 2)
+    cosine_three = dot_right(expand, turns_three[:8])
+    sine_three = dot_right(expand, turns_three[8:])
     zero = jnp.zeros((8, 128), F32)
     for shift in range(5):
         for x in range(8):
@@ -271,6 +276,13 @@
         high, low = split(rows)
         shape_high[:, 128 * o : 128 * o + 128] = high
         shape_low[:, 128 * o : 128 * o + 128] = low
+    pad = jnp.zeros((8, 64), F32)
+    angles = jnp.concatenate([rims[0, :, 32:64], angles_two, rims[1, :, 32:64], pad], axis=1)
+    lane = iota((16, 256), 1)
+    kind = child_of_box(lane % 128) + 8 * (lane // 128)
+    phases = dot_left(cosines(angles).T[:192], onehot(iota((16, 256), 0) == kind))
+    cosine_two, sine_two = phases[:, :128], phases[:, 128:]
+    parent = onehot(parent_of_box(iota((16, 128), 1)) == iota((16, 128), 0))
     level_one = dot(shape_high[...], leaf[...]) + dot(shape_low[...], leaf[...])
     own = jnp.concatenate(
         [level_one[96 * c + 32 : 96 * c + 64, 128 * r : 128 * r + 128] for c in range(2) for r in range(2)],
@@ -293,13 +305,6 @@
     for e, copy in halo_copies[:2]:
         pl.when(has[e])(copy.start)
 
-    pad = jnp.zeros((8, 64), F32)
-    angles = jnp.concatenate([rims[0, :, 32:64], angles_two, rims[1, :, 32:64], pad], axis=1)
-    lane = iota((16, 256), 1)
-    kind = child_of_box(lane % 128) + 8 * (lane // 128)
-    phases = dot_left(cosines(angles).T[:192], onehot(iota((16, 256), 0) == kind))
-    cosine_two, sine_two = phases[:, :128], phases[:, 128:]
-    parent = onehot(parent_of_box(iota((16, 128), 1)) == iota((16, 128), 0))
     real = dot3(up_two, level_one[:96])
     imag = dot3(up_two, level_one[96:])
     parts = []
@@ -314,11 +319,6 @@
         pl.when(has[e])(copy.start)
     level_two = jnp.concatenate(parts, axis=0)
     upper = dot3(level_two, up_three)
-    turns_three = cosines(jnp.concatenate([shift_three[:, a, :] for a in range(8)], axis=1))
-    row, column = iota((16, 8), 0), iota((16, 8), 1)
-    expand = onehot(column == 4 * (row // 8) + 2 * (row // 4 % 2) + row % 2)
-    cosine_three = dot_right(expand, turns_three[:8])
-    sine_three = dot_right(expand, turns_three[8:])
     parts = []
     for c in range(2):
         for r in range(2):

time: 53.9 us -> 53.4 us (level)
  the two profiles are of different devices: /device:TPU:32 before, /device:TPU:2 now
where the time goes in v8:
time: 53.4 us; the launch traced here: 53.2 us
  Pallas kernels  51.7 us (97%)
  local copies, waits for them, and re-layouts  1.47 us (3%)
    pallas_call x1, Pallas kernels, shards(): pl.pallas_call(functools.partial(whole, dirs, boxes), out_shape=jax.Shape...  51.7 us
    unnamed x1, local copies, waits for them, and re-layouts  1.47 us

profile of v8, /device:TPU:2, one launch (start us, length us, event | category | flops | bytes accessed | tf_op | source)
XLA Modules:
  0.0 53.2 jit_solution(5469099325238673106)
XLA Ops:
  0.0 51.7 %shard_map.163 = f32[8,2,8,128]{3,2,1,0:T(8,128)} custom-call(bf16[2048,128]{1,0:T(8,128)(2,1)} %bitcast.19, bf16[216,64]{1,0:T(8,128)(2,1)} %bitcast.23, s32[27,8,128]{2,1,0:T(8,128)} %refs_2_.1, bf16[2,8,64]{2,1,0:T(8,128)(2,1)} %bitcast.32, bf16[2,8,4,16]{3,2,1,0:T(4,128)(2,1)} %bitcast.26, f32[8,16]{1,0:T(8,128)} %bitcast.33, f32[16,32]{1,0:T(8,128)} %bitcast.29, ...), custom_call_target="tpu_custom_call" | custom-call | tf_op jit(solution)/shard_map/pallas_call | solution.py:586
  51.7 1.5 %copy.19 = f32[4,2,2,8,128]{4,3,2,1,0:T(8,128)} copy(f32[4,2,2,8,128]{4,3,2,1,0:T(8,128)} %bitcast.20) | data formatting | bytes 131072
